TPU v7x, 512 devices: a whole 4x8x8 slice. The times are simulated.
512 devices in a mesh: row: 32 (over x, z), col: 16 (over y, core).
Axes of the slice: x: 4, y: 8, z: 8, core: 2. Of those that a mesh axis runs over, the one named last changes fastest.
Arguments:
- qkv_grad: bfloat16 [8192, 18432], P('row', 'col'), may hold values from -2.5 to 2.5
- qkv_moment: bfloat16 [8192, 18432], P('row', 'col'), may hold values from -256 to 256
- qkv_basis: bfloat16 [18432, 256], P('col', 'row'), may hold values from -6 to 6
- out_grad: bfloat16 [8192, 16384], P('row', 'col'), may hold values from -2.5 to 2.5
- out_moment: bfloat16 [8192, 16384], P('row', 'col'), may hold values from -256 to 256
- out_basis: bfloat16 [16384, 256], P('col', 'row'), may hold values from -6 to 6
Outputs:
- qkv_moment_next: bfloat16 [8192, 18432], P('row', 'col')
- qkv_left: bfloat16 [8192, 256], P('row')
- qkv_right: bfloat16 [18432, 256], P('col', 'row')
- out_moment_next: bfloat16 [8192, 16384], P('row', 'col')
- out_left: bfloat16 [8192, 256], P('row')
- out_right: bfloat16 [16384, 256], P('col', 'row')
All inputs are finite; a program needn't handle non-finite values.
Results may differ from a plain program's by a relative error of at most 0.012.
Values may be sent and summed in bfloat16 or wider, within the bound.
No kernel may reach another device: no remote copies, remote signals or barrier semaphores. Data moves between devices by JAX's collectives and lax.ppermute only.
A program may use at most 64 MiB of HBM per device.

v0:
```python
import jax
import jax.numpy as jnp
from jax import lax
from jax.sharding import PartitionSpec as P

MOMENTUM_DECAY = 0.95
EPSILON = 1e-06


def combine_terms(moment_matrix, grad_matrix):
    return (moment_matrix.astype(jnp.float32) + grad_matrix.astype(jnp.float32)).astype(
        jnp.bfloat16
    )


def gram_of(projection):
    return jnp.dot(
        projection.T,
        projection,
        precision=lax.Precision.HIGHEST,
        preferred_element_type=jnp.float32,
    )


def orthonormal(projection, gram_matrix):
    factor = jnp.linalg.cholesky(gram_matrix)
    return jax.scipy.linalg.solve_triangular(factor, projection.T, lower=True).T.astype(
        jnp.bfloat16
    )


def transposed_product(combined, left_basis):
    return lax.dot_general(
        combined, left_basis, (((0,), (0,)), ((), ())), preferred_element_type=jnp.float32
    )


def finish_moment(combined, feedback, row_total):
    return (combined.astype(jnp.float32) - (1.0 - MOMENTUM_DECAY) / row_total * feedback).astype(
        jnp.bfloat16
    )


def per_device(qkv_grad, qkv_moment, qkv_basis, out_grad, out_moment, out_basis):
    qkv_combined = combine_terms(qkv_moment, qkv_grad)
    out_combined = combine_terms(out_moment, out_grad)
    row_total = qkv_combined.shape[0] * lax.axis_size("row")
    share_width = qkv_basis.shape[1]
    qkv_total = qkv_combined.shape[1] * lax.axis_size("col")
    out_total = out_combined.shape[1] * lax.axis_size("col")
    qkv_partial = jnp.dot(
        qkv_combined,
        lax.all_gather(qkv_basis, "row", axis=1, tiled=True),
        preferred_element_type=jnp.float32,
    )
    out_partial = jnp.dot(
        out_combined,
        lax.all_gather(out_basis, "row", axis=1, tiled=True),
        preferred_element_type=jnp.float32,
    )
    qkv_projection, out_projection = lax.psum((qkv_partial, out_partial), "col")
    qkv_gram, out_gram = lax.psum((gram_of(qkv_projection), gram_of(out_projection)), "row")
    qkv_left = orthonormal(qkv_projection, qkv_gram / row_total)
    out_left = orthonormal(out_projection, out_gram / row_total)
    qkv_terms = transposed_product(qkv_combined, qkv_left)
    out_terms = transposed_product(out_combined, out_left)
    qkv_coeff, out_coeff = lax.psum((qkv_terms, out_terms), "row")
    qkv_squares, out_squares = lax.psum(
        (jnp.sum(qkv_coeff * qkv_coeff, axis=0), jnp.sum(out_coeff * out_coeff, axis=0)), "col"
    )
    offset = lax.axis_index("row") * share_width
    qkv_own = lax.dynamic_slice_in_dim(qkv_coeff, offset, share_width, 1)
    out_own = lax.dynamic_slice_in_dim(out_coeff, offset, share_width, 1)
    qkv_scale = jnp.sqrt(
        lax.dynamic_slice_in_dim(qkv_squares, offset, share_width, 0) / qkv_total + EPSILON
    )
    out_scale = jnp.sqrt(
        lax.dynamic_slice_in_dim(out_squares, offset, share_width, 0) / out_total + EPSILON
    )
    qkv_right = (qkv_own / qkv_scale[None, :]).astype(jnp.bfloat16)
    out_right = (out_own / out_scale[None, :]).astype(jnp.bfloat16)
    qkv_low = qkv_coeff.astype(jnp.bfloat16)
    out_low = out_coeff.astype(jnp.bfloat16)
    qkv_feedback = lax.dot_general(
        qkv_left, qkv_low, (((1,), (1,)), ((), ())), preferred_element_type=jnp.float32
    )
    out_feedback = lax.dot_general(
        out_left, out_low, (((1,), (1,)), ((), ())), preferred_element_type=jnp.float32
    )
    qkv_next = finish_moment(qkv_combined, qkv_feedback, row_total)
    out_next = finish_moment(out_combined, out_feedback, row_total)
    return (qkv_next, qkv_left, qkv_right, out_next, out_left, out_right)


def solution(mesh):
    placed = (
        P("row", "col"),
        P("row", "col"),
        P("col", "row"),
        P("row", "col"),
        P("row", "col"),
        P("col", "row"),
    )
    return jax.shard_map(
        per_device,
        mesh=mesh,
        in_specs=placed,
        out_specs=(
            P("row", "col"),
            P("row", None),
            P("col", "row"),
            P("row", "col"),
            P("row", None),
            P("col", "row"),
        ),
        check_vma=False,
    )
```

profile of v0, /device:TPU:1, one launch (start us, length us, event | category | flops | bytes accessed | tf_op | source)
XLA Modules:
  0.0 720.2 jit_solution(14375837425858827175)
XLA Ops:
  7.2 44.6 %all_gather.6 = bf16[1152,256]{0,1:T(8,128)(2,1)S(1)} all-gather(bf16[1152,8]{0,1:T(8,128)(2,1)} %param.11), channel_id=1, replica_groups=mesh['row'=32,'col'=16] {'row'}, dimensions={1}, use_global_device_ids=true | all-gather | bytes 608256 | tf_op jit(solution)/shard_map/all_gather | solution.py:53
  51.8 37.1 %all_gather.7 = bf16[1024,256]{0,1:T(8,128)(2,1)S(1)} all-gather(bf16[1024,8]{0,1:T(8,128)(2,1)} %param.14), channel_id=1, replica_groups=mesh['row'=32,'col'=16] {'row'}, dimensions={1}, use_global_device_ids=true | all-gather | bytes 540672 | tf_op jit(solution)/shard_map/all_gather | solution.py:58
  89.0 2.2 fusion.27
  91.1 1.0 fusion.26
  92.3 134.7 %all-reduce.13.cloned.1.call-done = (f32[256,256]{1,0:T(8,128)}, f32[256,256]{1,0:T(8,128)}) async-done(((f32[256,256]{1,0:T(8,128)}, f32[256,256]{1,0:T(8,128)}), (f32[256,256]{1,0:T(8,128)}, f32[256,256]{1,0:T(8,128)})) %all-reduce.13.cloned.1.call-update) | async-done | bytes 524304 | tf_op jit(solution)/shard_map/psum | solution.py:61
  226.9 2.3 fusion.30
  229.2 2.3 fusion.31
  231.6 0.2 all-reduce.9.cloned.1.call-start
  231.8 155.5 %all-reduce.11.cloned.1.call-done = (f32[256,256]{0,1:T(8,128)}, f32[256,256]{0,1:T(8,128)}) async-done(((f32[256,256]{0,1:T(8,128)}, f32[256,256]{0,1:T(8,128)}), (f32[256,256]{0,1:T(8,128)}, f32[256,256]{0,1:T(8,128)})) %all-reduce.11.cloned.1.call-update) | async-done | bytes 524304 | tf_op jit(solution)/shard_map/psum | solution.py:62
  387.3 1.0 broadcast_multiply_fusion.1
  388.4 0.1 copy.13
  388.5 0.1 copy.15
  388.7 0.1 fusion.6
  388.8 11.7 %cholesky.164 = f32[128,128]{1,0:T(8,128)S(1)} custom-call(f32[128,128]{1,0:T(8,128)S(1)} %cholesky.197), custom_call_target="Cholesky" | custom-call | tf_op jit(solution)/shard_map/jit(cholesky)/cholesky | solution.py:26
  400.5 9.8 %custom-call.15 = f32[1,128,128]{1,2,0:T(8,128)S(1)} custom-call(f32[1,128,128]{2,1,0:T(8,128)S(1)} %get-tuple-element.61), custom_call_target="InvertDiagBlocksLowerTriangular" | custom-call | tf_op jit(solution)/shard_map/jit(cholesky)/cholesky | solution.py:26
  410.4 0.2 constant_dynamic-update-slice_fusion.1
  410.6 0.3 convolution_subtract_fusion.2
  410.8 11.7 %cholesky.181 = f32[128,128]{1,0:T(8,128)S(1)} custom-call(f32[128,128]{1,0:T(8,128)S(1)} %convolution_subtract_fusion.2), custom_call_target="Cholesky" | custom-call | tf_op jit(solution)/shard_map/jit(cholesky)/cholesky | solution.py:26
  422.6 0.6 compare_reduce_fusion
  423.2 0.6 compare_reduce_fusion.1
  425.2 0.1 triangular_solve.75
  425.3 4.0 while.5
  425.3 0.6 fusion.49
  425.9 1.4 bitcast_dynamic-update-slice_fusion.5
  427.3 0.6 fusion.49
  427.9 1.4 bitcast_dynamic-update-slice_fusion.5
  429.3 19.9 %custom-call.16 = f32[2,128,128]{1,2,0:T(8,128)S(1)} custom-call(f32[2,128,128]{2,1,0:T(8,128)S(1)} %get-tuple-element.23), custom_call_target="InvertDiagBlocksLowerTriangular" | custom-call | tf_op jit(solution)/shard_map/jit(_solve_triangular)/triangular_solve | solution.py:27
  449.2 0.3 fusion.8
  449.5 0.4 convolution_subtract_fusion
  449.9 0.3 fusion.13
  450.3 1.3 fusion.23
  451.6 11.7 %cholesky.130 = f32[128,128]{1,0:T(8,128)S(1)} custom-call(f32[128,128]{1,0:T(8,128)S(1)} %cholesky.194), custom_call_target="Cholesky" | custom-call | tf_op jit(solution)/shard_map/jit(cholesky)/cholesky | solution.py:26
  463.4 9.8 %custom-call.13 = f32[1,128,128]{1,2,0:T(8,128)S(1)} custom-call(f32[1,128,128]{2,1,0:T(8,128)S(1)} %get-tuple-element.65), custom_call_target="InvertDiagBlocksLowerTriangular" | custom-call | tf_op jit(solution)/shard_map/jit(cholesky)/cholesky | solution.py:26
  473.2 0.2 constant_dynamic-update-slice_fusion.3
  473.4 0.3 convolution_subtract_fusion.3
  473.7 11.7 %cholesky.147 = f32[128,128]{1,0:T(8,128)S(1)} custom-call(f32[128,128]{1,0:T(8,128)S(1)} %convolution_subtract_fusion.3), custom_call_target="Cholesky" | custom-call | tf_op jit(solution)/shard_map/jit(cholesky)/cholesky | solution.py:26
  485.4 0.6 compare_reduce_fusion.2
  486.1 0.6 compare_reduce_fusion.3
  488.1 4.0 while.4
  488.1 0.6 fusion.48
  488.7 1.4 bitcast_dynamic-update-slice_fusion.4
  490.1 0.6 fusion.48
  490.7 1.4 bitcast_dynamic-update-slice_fusion.4
  492.1 19.9 %custom-call.14 = f32[2,128,128]{1,2,0:T(8,128)S(1)} custom-call(f32[2,128,128]{2,1,0:T(8,128)S(1)} %get-tuple-element.22), custom_call_target="InvertDiagBlocksLowerTriangular" | custom-call | tf_op jit(solution)/shard_map/jit(_solve_triangular)/triangular_solve | solution.py:27
  512.0 0.3 fusion.10
  512.4 0.4 convolution_subtract_fusion.1
  512.8 0.3 fusion.17
  513.1 1.4 fusion.25
  514.6 0.8 copy.18
  515.4 0.8 copy.16
  516.1 162.1 %all-reduce.9.cloned.1.call-done = (f32[1152,256]{1,0:T(8,128)}, f32[1024,256]{1,0:T(8,128)}) async-done(((f32[1152,256]{1,0:T(8,128)}, f32[1024,256]{1,0:T(8,128)}), (f32[1152,256]{1,0:T(8,128)}, f32[1024,256]{1,0:T(8,128)})) %all-reduce.9.cloned.1.call-update) | async-done | bytes 2228240 | tf_op jit(solution)/shard_map/psum | solution.py:67
  678.2 1.5 multiply_reduce_fusion.1
  679.7 0.1 copy-done.1
  679.8 2.5 fusion.3
  682.2 0.2 multiply_reduce_fusion
  682.4 0.7 copy-done.7
  683.1 1.2 fusion.1
  684.3 27.2 %all-reduce.3 = (f32[256]{0:T(256)S(1)}, f32[256]{0:T(256)S(1)}) all-reduce(f32[256]{0:T(256)S(1)} %multiply_reduce_fusion, f32[256]{0:T(256)S(1)} %multiply_reduce_fusion.1), channel_id=1, replica_groups=mesh['row'=32,'col'=16] {'col'}, use_global_device_ids=true, to_apply=%region_8.0 | all-reduce | flops 512 | bytes 4096 | tf_op jit(solution)/shard_map/psum | solution.py:68
  711.5 0.1 add_sqrt_fusion
  711.6 0.2 divide_convert_fusion.1
  711.8 0.7 copy.19
  712.6 0.1 add_sqrt_fusion.1
  712.6 0.2 divide_convert_fusion
  712.9 0.8 copy.17
  (53 shorter events, 0.5 us)
Async XLA Ops:
  7.2 81.8 %copy-start.2 = (bf16[256,1152]{1,0:T(8,128)(2,1)S(1)}, bf16[256,1152]{1,0:T(8,128)(2,1)}, u32[]{:S(2)}) copy-start(bf16[256,1152]{1,0:T(8,128)(2,1)} %param.9) | copy-start | bytes 1769476
  7.2 219.7 %all-reduce.13.cloned.1.call-start = ((), (), s32[]{:S(2)}) async-start(), calls=%async_computation.2 | async-start | bytes 1048576 | tf_op jit(solution)/shard_map/psum | solution.py:61
  51.8 39.3 %copy-start.4 = (bf16[256,1024]{1,0:T(8,128)(2,1)S(1)}, bf16[256,1024]{1,0:T(8,128)(2,1)}, u32[]{:S(2)}) copy-start(bf16[256,1024]{1,0:T(8,128)(2,1)} %param.12) | copy-start | bytes 1572868
  51.8 39.3 %copy-start.5 = (bf16[256,1024]{1,0:T(8,128)(2,1)S(1)}, bf16[256,1024]{1,0:T(8,128)(2,1)}, u32[]{:S(2)}) copy-start(bf16[256,1024]{1,0:T(8,128)(2,1)} %param.13) | copy-start | bytes 1572868
  92.2 295.1 %all-reduce.11.cloned.1.call-start = ((), (), s32[]{:S(2)}) async-start(), calls=%async_computation.1 | async-start | bytes 1048576 | tf_op jit(solution)/shard_map/psum | solution.py:62
  231.6 446.6 %all-reduce.9.cloned.1.call-start = ((), (), s32[]{:S(2)}) async-start(), calls=%async_computation | async-start | bytes 4456448 | tf_op jit(solution)/shard_map/psum | solution.py:67
  387.3 1.2 copy-start.14
  387.3 1.4 copy-start.13
  410.3 38.9 %copy-start.9 = (f32[256,256]{1,0:T(8,128)S(1)}, f32[256,256]{1,0:T(8,128)}, u32[]{:S(2)}) copy-start(f32[256,256]{1,0:T(8,128)} %get-tuple-element.53) | copy-start | bytes 786436
  450.2 64.3 %copy-start.10 = (bf16[128,256]{1,0:T(8,128)(2,1)}, bf16[128,256]{1,0:T(8,128)(2,1)S(1)}, u32[]{:S(2)}) copy-start(bf16[128,256]{1,0:T(8,128)(2,1)S(1)} %fusion.13) | copy-start | bytes 196612
  473.2 38.9 %copy-start.8 = (f32[256,256]{1,0:T(8,128)S(1)}, f32[256,256]{1,0:T(8,128)}, u32[]{:S(2)}) copy-start(f32[256,256]{1,0:T(8,128)} %get-tuple-element.52) | copy-start | bytes 786436
  488.0 25.1 %copy-start.3 = (bf16[256,1152]{1,0:T(8,128)(2,1)S(1)}, bf16[256,1152]{1,0:T(8,128)(2,1)}, u32[]{:S(2)}) copy-start(bf16[256,1152]{1,0:T(8,128)(2,1)} %param.10) | copy-start | bytes 1769476
  512.4 3.0 copy-start.6
  513.1 2.3 copy-start.11
  678.2 1.5 copy-start.1
  679.8 2.5 copy-start
  682.2 0.9 copy-start.7
  682.2 0.9 copy-start.12
Sparse Core Ops, SparseCore 0:
  92.3 134.5 all-reduce.12
  231.7 155.5 all-reduce.10
  514.7 163.4 all-reduce.8
where the time goes:
time: 721 us; the launch traced here: 720 us
  waiting for transfers between devices  452 us (63%)
  other arithmetic  112 us (16%)
  blocking collectives  109 us (15%)
  matrix products  17.3 us (2%)
  between operations  16.7 us (2%)
  local copies, waits for them, and re-layouts  12.2 us (2%)
    psum x1, waiting for transfers between devices, per_device(): qkv_coeff, out_coeff = lax.psum((qkv_terms, out_terms), 'row')  162 us
    psum x1, waiting for transfers between devices, per_device(): lax.psum((gram_of(qkv_projection), gram_of(out_projection)), 'row')  155 us
    psum x1, waiting for transfers between devices, per_device(): qkv_projection, out_projection = lax.psum((qkv_partial, out_partial), 'col')  135 us
    another operation x14, other arithmetic, orthonormal(): factor = jnp.linalg.cholesky(gram_matrix)  69.2 us
    all_gather x1, blocking collectives, per_device(): lax.all_gather(qkv_basis, 'row', axis=1, tiled=True)  44.6 us
    another operation x5, other arithmetic, orthonormal(): jax.scipy.linalg.solve_triangular(factor, projection.T, lower=True)  39.9 us
    all_gather x1, blocking collectives, per_device(): lax.all_gather(out_basis, 'row', axis=1, tiled=True)  37.1 us
    psum x1, blocking collectives, per_device(): lax.psum((jnp.sum(qkv_coeff * qkv_coeff, axis=0), jnp.sum(out_coeff * out...  27.2 us
  transfers between devices with their start and end apart: 3, of which 3 were waited for; matrix products, arithmetic and copies ran while one was open for 0% of the time, Pallas kernels for 0%

commit v1 on v0

v1 whole, which is shorter than its diff:
```python
import functools

import jax
import jax.numpy as jnp
from jax import lax
from jax.experimental import pallas as pl
from jax.experimental.pallas import tpu as pltpu
from jax.sharding import PartitionSpec as P

MOMENTUM_DECAY = 0.95
EPSILON = 1e-06
PANEL = 16
LANES = 128
CORES = 2


def combine_terms(moment_matrix, grad_matrix):
    return (moment_matrix.astype(jnp.float32) + grad_matrix.astype(jnp.float32)).astype(
        jnp.bfloat16
    )


def split_terms(value):
    high = value.astype(jnp.bfloat16)
    rest = value - high.astype(jnp.float32)
    middle = rest.astype(jnp.bfloat16)
    low = (rest - middle.astype(jnp.float32)).astype(jnp.bfloat16)
    return high, middle, low


def whiten_kernel(row_total, gram_ref, proj_ref, left_ref, work_ref):
    size = gram_ref.shape[0]
    rows = proj_ref.shape[0]
    width = size + rows
    work_ref[:, :size] = gram_ref[...] * (1.0 / row_total)
    work_ref[:, size:] = proj_ref[...].T
    row = lax.broadcasted_iota(jnp.int32, (PANEL, LANES), 0)
    for start in range(0, size, PANEL):
        stop = start + PANEL
        base = start // LANES * LANES
        panel = [work_ref[start:stop, at : at + LANES] for at in range(base, width, LANES)]
        columns = [
            jnp.broadcast_to(panel[0][:, at : at + 1], (PANEL, LANES))
            for at in range(start - base, stop - base)
        ]
        pivots = jnp.ones((PANEL, LANES), jnp.float32)
        for step in range(PANEL):
            pivot = jnp.broadcast_to(columns[step][step : step + 1, :], (PANEL, LANES))
            pivots = jnp.where(row == step, pivot, pivots)
            if step == PANEL - 1:
                break
            ratio = jnp.where(row > step, columns[step] * (1.0 / pivot), 0.0)
            for other in range(step + 1, PANEL):
                columns[other] = columns[other] - ratio * columns[other][step : step + 1, :]
            panel = [block - ratio * block[step : step + 1, :] for block in panel]
        scale = lax.rsqrt(pivots)
        scale = scale * (1.5 - 0.5 * pivots * scale * scale)
        panel = [block * scale for block in panel]
        done = (size - base) // LANES
        for at in range(rows // LANES):
            work_ref[start:stop, size + at * LANES : size + (at + 1) * LANES] = panel[done + at]
        if stop < size:
            later = stop // LANES * LANES
            high, middle, low = split_terms(
                jnp.concatenate(panel[(later - base) // LANES :], axis=1)
            )
            keep = size - later
            lhs = jnp.concatenate(
                [part[:, :keep] for part in (high, high, high, middle, middle, low)], axis=0
            )
            rhs = jnp.concatenate([high, middle, low, high, middle, high], axis=0)
            update = lax.dot_general(
                lhs, rhs, (((0,), (0,)), ((), ())), preferred_element_type=jnp.float32
            )
            work_ref[stop:size, later:] = work_ref[stop:size, later:] - update[stop - later :, :]
    left_ref[...] = work_ref[:, size:].T.astype(left_ref.dtype)


def whiten(gram_sum, projection, row_total):
    size = gram_sum.shape[0]
    rows = projection.shape[0]
    return pl.pallas_call(
        functools.partial(whiten_kernel, float(row_total)),
        out_shape=jax.ShapeDtypeStruct((rows, size), jnp.bfloat16),
        in_specs=[pl.BlockSpec(memory_space=pltpu.VMEM)] * 2,
        out_specs=pl.BlockSpec(memory_space=pltpu.VMEM),
        scratch_shapes=[pltpu.VMEM((size, size + rows), jnp.float32)],
        compiler_params=pltpu.CompilerParams(vmem_limit_bytes=32 * 2**20),
    )(gram_sum, projection)


def exchange(blocks, axis, groups=None):
    return lax.all_to_all(blocks, axis, 0, 0, axis_index_groups=groups)


def gather(block, axis, count, groups=None):
    return exchange(jnp.broadcast_to(block[None], (count, *block.shape)), axis, groups)


def scatter_sum(blocks, axis, groups=None):
    return jnp.sum(exchange(blocks, axis, groups).astype(jnp.float32), axis=0)


def per_device(qkv_grad, qkv_moment, qkv_basis, out_grad, out_moment, out_basis):
    row_count = lax.axis_size("row")
    col_count = lax.axis_size("col")
    chips = col_count // CORES
    same_core = [[chip * CORES + core for chip in range(chips)] for core in range(CORES)]
    same_chip = [[chip * CORES + core for core in range(CORES)] for chip in range(chips)]
    local_rows, qkv_width = qkv_grad.shape
    width = qkv_width + out_grad.shape[1]
    row_total = local_rows * row_count
    share = qkv_basis.shape[1]
    rank = share * row_count
    qkv_total = qkv_width * col_count
    out_total = (width - qkv_width) * col_count

    with jax.named_scope("basis_gather"):
        basis = jnp.concatenate([qkv_basis.T, out_basis.T], axis=1)
        basis = gather(basis, "row", row_count).reshape(rank, width)
    with jax.named_scope("projection_partial"):
        qkv_combined = combine_terms(qkv_moment, qkv_grad)
        out_combined = combine_terms(out_moment, out_grad)
        partial = [
            lax.dot_general(
                combined,
                part,
                (((1,), (1,)), ((), ())),
                preferred_element_type=jnp.float32,
            ).reshape(chips, local_rows // chips, rank)
            for combined, part in (
                (qkv_combined, basis[:, :qkv_width]),
                (out_combined, basis[:, qkv_width:]),
            )
        ]
        partial = jnp.stack(partial, axis=1).reshape(col_count, local_rows // chips, rank)
    with jax.named_scope("projection_sum"):
        own = scatter_sum(partial, "col")
        projection = gather(own, "col", chips, same_core).reshape(local_rows, rank)
    with jax.named_scope("gram_sum"):
        gram = jnp.dot(
            projection.T,
            projection,
            precision=lax.Precision.HIGHEST,
            preferred_element_type=jnp.float32,
        )
        gram = scatter_sum(gram.reshape(row_count, share, rank), "row")
        gram = gather(gram, "row", row_count).reshape(rank, rank)
    with jax.named_scope("whiten"):
        left = whiten(gram, projection, row_total)
        left = gather(left, "col", CORES, same_chip)
    qkv_left, out_left = left[0], left[1]
    with jax.named_scope("coefficients"):
        terms = [
            lax.dot_general(
                part, combined, (((0,), (0,)), ((), ())), preferred_element_type=jnp.float32
            ).astype(jnp.bfloat16)
            for part, combined in ((qkv_left, qkv_combined), (out_left, out_combined))
        ]
        terms = jnp.concatenate(terms, axis=1).reshape(row_count, share, width)
        coeff = scatter_sum(terms, "row")
    with jax.named_scope("coefficient_gather"):
        low = gather(coeff.astype(jnp.bfloat16), "row", row_count).reshape(rank, width)
    with jax.named_scope("squares"):
        squared = coeff * coeff
        lane = lax.broadcasted_iota(jnp.int32, (share, LANES), 1)
        squares = jnp.where(
            lane < LANES // 2,
            jnp.sum(squared[:, :qkv_width], axis=1, keepdims=True),
            jnp.sum(squared[:, qkv_width:], axis=1, keepdims=True),
        )
        squares = jnp.sum(gather(squares, "col", col_count), axis=0)
        qkv_scale = jnp.sqrt(squares[:, :1] / qkv_total + EPSILON)
        out_scale = jnp.sqrt(squares[:, LANES // 2 : LANES // 2 + 1] / out_total + EPSILON)
        qkv_right = (coeff[:, :qkv_width] / qkv_scale).astype(jnp.bfloat16).T
        out_right = (coeff[:, qkv_width:] / out_scale).astype(jnp.bfloat16).T
    with jax.named_scope("moment_next"):
        nexts = [
            (
                combined.astype(jnp.float32)
                - (1.0 - MOMENTUM_DECAY)
                / row_total
                * jnp.dot(part, part_low, preferred_element_type=jnp.float32)
            ).astype(jnp.bfloat16)
            for combined, part, part_low in (
                (qkv_combined, qkv_left, low[:, :qkv_width]),
                (out_combined, out_left, low[:, qkv_width:]),
            )
        ]
    return (nexts[0], qkv_left, qkv_right, nexts[1], out_left, out_right)


def solution(mesh):
    placed = (
        P("row", "col"),
        P("row", "col"),
        P("col", "row"),
        P("row", "col"),
        P("row", "col"),
        P("col", "row"),
    )
    return jax.shard_map(
        per_device,
        mesh=mesh,
        in_specs=placed,
        out_specs=(
            P("row", "col"),
            P("row", None),
            P("col", "row"),
            P("row", "col"),
            P("row", None),
            P("col", "row"),
        ),
        check_vma=False,
    )
```

time: 721 us -> 218 us (0.30)
  waiting for transfers between devices: 452 us -> 51 us
  other arithmetic: 112 us -> 4.01 us
  blocking collectives: 109 us -> 136 us
  between operations: 16.7 us -> 0.8 us
  matrix products: 17.3 us -> 4.1 us
  local copies, waits for them, and re-layouts: 12.2 us -> 2.27 us
  starting transfers between devices: 0.3 us -> 9.05 us
  Pallas kernels: 0 us -> 7.62 us
    psum x3 -> x0, waiting for transfers between devices: 452 us -> none  [the longest x1 162 us: per_device(): qkv_coeff, out_coeff = lax.psum((qkv_terms, out_terms), 'row')]
    all_to_all x0 -> x7, blocking collectives: none -> 136 us  [exchange(): return lax.all_to_all(blocks, axis, 0, 0, axis_index_groups=groups)]
    another operation x19 -> x1, other arithmetic: 109 us -> 0.04 us  [per_device(): jnp.stack(partial, axis=1).reshape(col_count, local_rows // chips, rank)]
    all_gather x2 -> x0, blocking collectives: 81.7 us -> none  [the longest x1 44.6 us: per_device(): lax.all_gather(qkv_basis, 'row', axis=1, tiled=True)]
    all_to_all x0 -> x2, waiting for transfers between devices: none -> 51 us  [exchange(): return lax.all_to_all(blocks, axis, 0, 0, axis_index_groups=groups)]
    psum x1 -> x0, blocking collectives: 27.2 us -> none  [per_device(): lax.psum((jnp.sum(qkv_coeff * qkv_coeff, axis=0), jnp.sum(out_coeff * out...]
    dot_general x8 -> x7, matrix products: 14.3 us -> 4.1 us  [the longest x2 2.29 us: per_device(): jnp.dot(part, part_low, preferred_element_type=jnp.float32)]
    all_to_all x0 -> x2, starting transfers between devices: none -> 9.05 us  [exchange(): return lax.all_to_all(blocks, axis, 0, 0, axis_index_groups=groups)]
  transfers between devices with their start and end apart: 3 -> 2, of which waited for: 3 -> 2; matrix products, arithmetic and copies ran while one was open for 0% -> 1% of each run, Pallas kernels for 0% -> 0%
where the time goes in v1:
time: 218 us; the launch traced here: 215 us
  blocking collectives  136 us (62%)
  waiting for transfers between devices  51 us (23%)
  starting transfers between devices  9.05 us (4%)
  Pallas kernels  7.62 us (3%)
  matrix products  4.1 us (2%)
  other arithmetic  4.01 us (2%)
  local copies, waits for them, and re-layouts  2.27 us (1%)
    all_to_all x7, blocking collectives, exchange(): return lax.all_to_all(blocks, axis, 0, 0, axis_index_groups=groups)  136 us
    all_to_all x2, waiting for transfers between devices, exchange(): return lax.all_to_all(blocks, axis, 0, 0, axis_index_groups=groups)  51 us
    all_to_all x2, starting transfers between devices, exchange(): return lax.all_to_all(blocks, axis, 0, 0, axis_index_groups=groups)  9.05 us
    pallas_call x1, Pallas kernels, whiten(): pl.pallas_call(functools.partial(whiten_kernel, float(row_total)), out_sh...  7.62 us
  transfers between devices with their start and end apart: 2, of which 2 were waited for; matrix products, arithmetic and copies ran while one was open for 1% of the time, Pallas kernels for 0%

profile of v1, /device:TPU:1, one launch (start us, length us, event | category | flops | bytes accessed | tf_op | source)
XLA Modules:
  0.0 214.8 jit_solution(14583483882838046679)
XLA Ops:
  0.6 0.7 pad_maximum_fusion.1
  1.4 0.1 broadcast_in_dim.22
  1.5 0.0 copy-start
  1.5 0.0 copy-start.1
  1.5 44.0 %all_to_all.45 = bf16[32,8,2176]{2,1,0:T(8,128)(2,1)S(1)} all-to-all(bf16[32,8,2176]{2,1,0:T(8,128)(2,1)S(1)} %broadcast_in_dim.22), channel_id=1, replica_groups=mesh['row'=32,'col'=16] {'row'}, dimensions={0} | all-to-all | bytes 2228224 | tf_op jit(solution)/shard_map/basis_gather/all_to_all | solution.py:93
  45.5 0.0 copy-start.2
  45.5 0.0 copy-start.3
  45.5 0.0 copy-done
  45.5 0.0 copy-done.1
  45.5 0.3 fusion.8
  45.9 0.7 copy-done.2
  46.6 0.2 copy-done.3
  46.8 0.4 fusion.5
  47.2 26.5 %all_to_all.46 = f32[16,32,256]{2,1,0:T(8,128)S(1)} all-to-all(f32[16,32,256]{2,1,0:T(8,128)S(1)} %bitcast.43), channel_id=1, replica_groups=mesh['row'=32,'col'=16] {'col'}, dimensions={0} | all-to-all | bytes 1048576 | tf_op jit(solution)/shard_map/projection_sum/all_to_all | solution.py:93
  73.8 14.8 %all_to_all.47 = f32[8,32,256]{2,1,0:T(8,128)S(1)} all-to-all(f32[8,32,256]{2,1,0:T(8,128)S(1)} %broadcast_in_dim.23), channel_id=1, replica_groups={{0,2,4,6,8,10,12,14},{1,3,5,7,9,11,13,15},{16,18,20,22,24,26,28,30},{17..., dimensions={0} | all-to-all | bytes 524288 | tf_op jit(solution)/shard_map/projection_sum/all_to_all | solution.py:93
  88.5 0.1 copy.21
  88.7 0.4 fusion.10
  89.0 12.7 %all_to_all.48 = f32[32,8,256]{2,1,0:T(8,128)S(1)} all-to-all(f32[32,8,256]{2,1,0:T(8,128)S(1)} %fusion.10), channel_id=1, replica_groups=mesh['row'=32,'col'=16] {'row'}, dimensions={0} | all-to-all | bytes 524288 | tf_op jit(solution)/shard_map/gram_sum/all_to_all | solution.py:93
  101.8 15.9 %all_to_all.49 = f32[32,8,256]{2,1,0:T(8,128)S(1)} all-to-all(f32[32,8,256]{2,1,0:T(8,128)S(1)} %broadcast_in_dim.24), channel_id=1, replica_groups=mesh['row'=32,'col'=16] {'row'}, dimensions={0} | all-to-all | bytes 524288 | tf_op jit(solution)/shard_map/gram_sum/all_to_all | solution.py:93
  117.7 7.6 %whiten.1 = bf16[256,256]{1,0:T(8,128)(2,1)S(1)} custom-call(f32[256,256]{1,0:T(8,128)S(1)} %bitcast.38, f32[256,256]{1,0:T(8,128)S(1)} %bitcast.37), custom_call_target="tpu_custom_call" | custom-call | tf_op jit(solution)/shard_map/whiten/pallas_call | solution.py:82
  125.3 7.3 %all_to_all.50 = bf16[2,256,256]{2,1,0:T(8,128)(2,1)S(1)} all-to-all(bf16[2,256,256]{2,1,0:T(8,128)(2,1)S(1)} %broadcast_in_dim.25), channel_id=1, replica_groups={{0,1},{2,3},{4,5},{6,7},{8,9},{10,11},{12,13},{14,15},{16,17},{18,19},{..., dimensions={0} | all-to-all | bytes 524288 | tf_op jit(solution)/shard_map/whiten/all_to_all | solution.py:93
  132.6 0.0 copy-start.5
  132.7 0.0 copy-start.6
  132.7 0.3 convolution_convert_fusion.1
  133.0 0.4 convolution_convert_fusion
  133.4 1.1 maximum_bitcast_fusion
  134.5 4.2 %all-to-all-start.6 = ((bf16[32,8,2176]{2,1,0:T(8,128)(2,1)}), bf16[32,8,2176]{2,1,0:T(8,128)(2,1)S(1)}, u32[]{:S(2)}, u32[]{:S(2)}) async-start(bf16[32,8,2176]{2,1,0:T(8,128)(2,1)} %maximum_bitcast_fusion), calls=%async_computation.6 | async-start | bytes 2228224 | tf_op jit(solution)/shard_map/coefficients/all_to_all | solution.py:93
  138.7 26.3 %all-to-all-done.6 = bf16[32,8,2176]{2,1,0:T(8,128)(2,1)S(1)} async-done(((bf16[32,8,2176]{2,1,0:T(8,128)(2,1)}), bf16[32,8,2176]{2,1,0:T(8,128)(2,1)S(1)}, u32[]{:S(2)}, u32[]{:S(2)}) %all-to-all-start.6) | async-done | bytes 1114144 | tf_op jit(solution)/shard_map/coefficients/all_to_all | solution.py:93
  165.0 0.2 convert_reduce_fusion
  165.1 0.1 slice_reduce_fusion.1
  165.3 0.1 slice_reduce_fusion
  165.4 0.1 broadcast_select_fusion
  165.5 14.8 %all_to_all.51 = f32[16,8,128]{2,1,0:T(8,128)S(1)} all-to-all(f32[16,8,128]{2,1,0:T(8,128)S(1)} %broadcast_in_dim.35), channel_id=1, replica_groups=mesh['row'=32,'col'=16] {'col'}, dimensions={0} | all-to-all | bytes 131072 | tf_op jit(solution)/shard_map/squares/all_to_all | solution.py:93
  180.3 1.1 broadcast_in_dim.26
  181.4 4.9 %all-to-all-start.7 = ((bf16[32,8,2176]{2,1,0:T(8,128)(2,1)}), bf16[32,8,2176]{2,1,0:T(8,128)(2,1)S(1)}, u32[]{:S(2)}, u32[]{:S(2)}) async-start(bf16[32,8,2176]{2,1,0:T(8,128)(2,1)} %broadcast_in_dim.26), calls=%async_computation.7 | async-start | bytes 2228224 | tf_op jit(solution)/shard_map/coefficient_gather/all_to_all | solution.py:93
  186.3 0.2 sqrt_reduce_fusion
  186.5 0.7 fusion.15
  187.2 0.7 fusion.14
  187.8 24.7 %all-to-all-done.7 = bf16[32,8,2176]{2,1,0:T(8,128)(2,1)S(1)} async-done(((bf16[32,8,2176]{2,1,0:T(8,128)(2,1)}), bf16[32,8,2176]{2,1,0:T(8,128)(2,1)S(1)}, u32[]{:S(2)}, u32[]{:S(2)}) %all-to-all-start.7) | async-done | bytes 1114144 | tf_op jit(solution)/shard_map/coefficient_gather/all_to_all | solution.py:93
  212.5 0.0 copy-done.5
  212.5 0.0 copy-start.4
  212.5 1.1 fusion.3
  213.6 0.0 copy-done.6
  213.6 0.0 copy-done.4
  213.6 1.2 fusion.1
  (11 shorter events, 0.2 us)
Async XLA Ops:
  1.5 44.1 %copy-start = (bf16[256,1024]{1,0:T(8,128)(2,1)S(1)}, bf16[256,1024]{1,0:T(8,128)(2,1)}, u32[]{:S(2)}) copy-start(bf16[256,1024]{1,0:T(8,128)(2,1)} %param.9) | copy-start | bytes 1572868
  1.5 44.1 %copy-start.1 = (bf16[256,1024]{1,0:T(8,128)(2,1)S(1)}, bf16[256,1024]{1,0:T(8,128)(2,1)}, u32[]{:S(2)}) copy-start(bf16[256,1024]{1,0:T(8,128)(2,1)} %param.10) | copy-start | bytes 1572868
  45.5 1.1 copy-start.2
  45.5 1.2 copy-start.3
  132.6 79.9 %copy-start.5 = (bf16[256,256]{1,0:T(8,128)(2,1)}, bf16[256,256]{1,0:T(8,128)(2,1)S(1)}, u32[]{:S(2)}) copy-start(bf16[256,256]{1,0:T(8,128)(2,1)S(1)} %get-tuple-element.8) | copy-start | bytes 393220
  132.7 81.0 %copy-start.6 = (bf16[256,256]{1,0:T(8,128)(2,1)}, bf16[256,256]{1,0:T(8,128)(2,1)S(1)}, u32[]{:S(2)}) copy-start(bf16[256,256]{1,0:T(8,128)(2,1)S(1)} %get-tuple-element.9) | copy-start | bytes 393220
  134.5 30.5 %all-to-all-start.6 = ((bf16[32,8,2176]{2,1,0:T(8,128)(2,1)}), bf16[32,8,2176]{2,1,0:T(8,128)(2,1)S(1)}, u32[]{:S(2)}, u32[]{:S(2)}) async-start(bf16[32,8,2176]{2,1,0:T(8,128)(2,1)} %maximum_bitcast_fusion), calls=%async_computation.6 | async-start | bytes 2228224 | tf_op jit(solution)/shard_map/coefficients/all_to_all | solution.py:93
  181.4 31.2 %all-to-all-start.7 = ((bf16[32,8,2176]{2,1,0:T(8,128)(2,1)}), bf16[32,8,2176]{2,1,0:T(8,128)(2,1)S(1)}, u32[]{:S(2)}, u32[]{:S(2)}) async-start(bf16[32,8,2176]{2,1,0:T(8,128)(2,1)} %broadcast_in_dim.26), calls=%async_computation.7 | async-start | bytes 2228224 | tf_op jit(solution)/shard_map/coefficient_gather/all_to_all | solution.py:93
  212.5 1.1 copy-start.4

commit v2 on v1

--- a/solution.py
+++ b/solution.py
@@ -12,6 +12,7 @@
 PANEL = 16
 LANES = 128
 CORES = 2
+DEPTH = 8
 
 
 def combine_terms(moment_matrix, grad_matrix):
@@ -107,6 +108,9 @@
     chips = col_count // CORES
     same_core = [[chip * CORES + core for chip in range(chips)] for core in range(CORES)]
     same_chip = [[chip * CORES + core for core in range(CORES)] for chip in range(chips)]
+    outer = row_count // DEPTH
+    along_z = [[x * DEPTH + z for z in range(DEPTH)] for x in range(outer)]
+    along_x = [[x * DEPTH + z for x in range(outer)] for z in range(DEPTH)]
     local_rows, qkv_width = qkv_grad.shape
     width = qkv_width + out_grad.shape[1]
     row_total = local_rows * row_count
@@ -117,7 +121,8 @@
 
     with jax.named_scope("basis_gather"):
         basis = jnp.concatenate([qkv_basis.T, out_basis.T], axis=1)
-        basis = gather(basis, "row", row_count).reshape(rank, width)
+        basis = gather(basis, "row", DEPTH, along_z).reshape(DEPTH * share, width)
+        basis = gather(basis, "row", outer, along_x).reshape(rank, width)
     with jax.named_scope("projection_partial"):
         qkv_combined = combine_terms(qkv_moment, qkv_grad)
         out_combined = combine_terms(out_moment, out_grad)
@@ -127,15 +132,17 @@
                 part,
                 (((1,), (1,)), ((), ())),
                 preferred_element_type=jnp.float32,
-            ).reshape(chips, local_rows // chips, rank)
+            )
             for combined, part in (
                 (qkv_combined, basis[:, :qkv_width]),
                 (out_combined, basis[:, qkv_width:]),
             )
         ]
-        partial = jnp.stack(partial, axis=1).reshape(col_count, local_rows // chips, rank)
+        partial = jnp.stack(partial)
     with jax.named_scope("projection_sum"):
-        own = scatter_sum(partial, "col")
+        own = scatter_sum(partial, "col", same_chip)
+        own = own.reshape(chips, local_rows // chips, rank)
+        own = scatter_sum(own, "col", same_core)
         projection = gather(own, "col", chips, same_core).reshape(local_rows, rank)
     with jax.named_scope("gram_sum"):
         gram = jnp.dot(
@@ -157,23 +164,29 @@
             ).astype(jnp.bfloat16)
             for part, combined in ((qkv_left, qkv_combined), (out_left, out_combined))
         ]
-        terms = jnp.concatenate(terms, axis=1).reshape(row_count, share, width)
-        coeff = scatter_sum(terms, "row")
-    with jax.named_scope("coefficient_gather"):
-        low = gather(coeff.astype(jnp.bfloat16), "row", row_count).reshape(rank, width)
+        terms = jnp.concatenate(terms, axis=1).reshape(outer, DEPTH * share, width)
+        terms = scatter_sum(terms, "row", along_x).astype(jnp.bfloat16)
+        coeff = scatter_sum(terms.reshape(DEPTH, share, width), "row", along_z)
     with jax.named_scope("squares"):
         squared = coeff * coeff
-        lane = lax.broadcasted_iota(jnp.int32, (share, LANES), 1)
-        squares = jnp.where(
-            lane < LANES // 2,
-            jnp.sum(squared[:, :qkv_width], axis=1, keepdims=True),
-            jnp.sum(squared[:, qkv_width:], axis=1, keepdims=True),
+        squares = jnp.concatenate(
+            [
+                jnp.broadcast_to(jnp.sum(part, axis=1, keepdims=True), (share, LANES // 2))
+                for part in (squared[:, :qkv_width], squared[:, qkv_width:])
+            ],
+            axis=1,
         )
         squares = jnp.sum(gather(squares, "col", col_count), axis=0)
         qkv_scale = jnp.sqrt(squares[:, :1] / qkv_total + EPSILON)
         out_scale = jnp.sqrt(squares[:, LANES // 2 : LANES // 2 + 1] / out_total + EPSILON)
         qkv_right = (coeff[:, :qkv_width] / qkv_scale).astype(jnp.bfloat16).T
         out_right = (coeff[:, qkv_width:] / out_scale).astype(jnp.bfloat16).T
+    with jax.named_scope("coefficient_gather"):
+        low, qkv_right, out_right = lax.optimization_barrier(
+            (coeff.astype(jnp.bfloat16), qkv_right, out_right)
+        )
+        low = gather(low, "row", DEPTH, along_z).reshape(DEPTH * share, width)
+        low = gather(low, "row", outer, along_x).reshape(rank, width)
     with jax.named_scope("moment_next"):
         nexts = [
             (

time: 218 us -> 207 us (0.950); the launches traced: 215 us -> 206 us
  blocking collectives: 136 us -> 189 us
  waiting for transfers between devices: 51 us -> 0 us
  starting transfers between devices: 9.05 us -> 0 us
    all_to_all x7 -> x13, blocking collectives: 136 us -> 189 us  [exchange(): return lax.all_to_all(blocks, axis, 0, 0, axis_index_groups=groups)]
    all_to_all x2 -> x0, waiting for transfers between devices: 51 us -> none  [exchange(): return lax.all_to_all(blocks, axis, 0, 0, axis_index_groups=groups)]
    all_to_all x2 -> x0, starting transfers between devices: 9.05 us -> none  [exchange(): return lax.all_to_all(blocks, axis, 0, 0, axis_index_groups=groups)]
  transfers between devices with their start and end apart: 2 -> 0, of which waited for: 2 -> 0; matrix products, arithmetic and copies ran while one was open for 1% -> 0% of each run, Pallas kernels for 0% -> 0%
where the time goes in v2:
time: 207 us; the launch traced here: 206 us
  blocking collectives  189 us (91%)
  Pallas kernels  7.62 us (4%)
  matrix products  4.11 us (2%)
  other arithmetic  3.11 us (2%)
    all_to_all x13, blocking collectives, exchange(): return lax.all_to_all(blocks, axis, 0, 0, axis_index_groups=groups)  189 us
    pallas_call x1, Pallas kernels, whiten(): pl.pallas_call(functools.partial(whiten_kernel, float(row_total)), out_sh...  7.62 us

profile of v2, /device:TPU:1, one launch (start us, length us, event | category | flops | bytes accessed | tf_op | source)
XLA Modules:
  0.0 206.4 jit_solution(8094968921388334918)
XLA Ops:
  0.6 0.7 pad_maximum_fusion.2
  1.4 21.3 %all_to_all.65 = bf16[8,8,2176]{2,1,0:T(8,128)(2,1)S(1)} all-to-all(bf16[8,8,2176]{2,1,0:T(8,128)(2,1)S(1)} %broadcast_in_dim.24), channel_id=1, replica_groups={{0,16,32,48,64,80,96,112},{128,144,160,176,192,208,224,240},{256,272,28..., dimensions={0} | all-to-all | bytes 557056 | tf_op jit(solution)/shard_map/basis_gather/all_to_all | solution.py:94
  22.7 0.1 broadcast_in_dim.26
  22.8 0.0 copy-start
  22.8 0.0 copy-start.1
  22.8 16.9 %all_to_all.66 = bf16[4,64,2176]{2,1,0:T(8,128)(2,1)S(1)} all-to-all(bf16[4,64,2176]{2,1,0:T(8,128)(2,1)S(1)} %broadcast_in_dim.26), channel_id=1, replica_groups={{0,128,256,384},{16,144,272,400},{32,160,288,416},{48,176,304,432},{64,..., dimensions={0} | all-to-all | bytes 2228224 | tf_op jit(solution)/shard_map/basis_gather/all_to_all | solution.py:94
  39.7 0.0 copy-start.2
  39.7 0.0 copy-start.3
  39.7 0.0 copy-done
  39.7 0.0 copy-done.1
  39.7 0.3 convolution_bitcast_fusion
  40.1 0.7 copy-done.2
  40.8 0.2 copy-done.3
  40.9 0.4 convolution_bitcast_fusion.1
  41.4 7.6 %all_to_all.67 = f32[2,256,256]{2,1,0:T(8,128)S(1)} all-to-all(f32[2,256,256]{2,1,0:T(8,128)S(1)} %pad_maximum_fusion.1), channel_id=1, replica_groups={{0,1},{2,3},{4,5},{6,7},{8,9},{10,11},{12,13},{14,15},{16,17},{18,19},{..., dimensions={0} | all-to-all | bytes 1048576 | tf_op jit(solution)/shard_map/projection_sum/all_to_all | solution.py:94
  49.0 17.7 %all_to_all.68 = f32[8,32,256]{2,1,0:T(8,128)S(1)} all-to-all(f32[8,32,256]{2,1,0:T(8,128)S(1)} %bitcast.47), channel_id=1, replica_groups={{0,2,4,6,8,10,12,14},{1,3,5,7,9,11,13,15},{16,18,20,22,24,26,28,30},{17..., dimensions={0} | all-to-all | bytes 524288 | tf_op jit(solution)/shard_map/projection_sum/all_to_all | solution.py:94
  66.7 12.1 %all_to_all.69 = f32[8,32,256]{2,1,0:T(8,128)S(1)} all-to-all(f32[8,32,256]{2,1,0:T(8,128)S(1)} %broadcast_in_dim.27), channel_id=1, replica_groups={{0,2,4,6,8,10,12,14},{1,3,5,7,9,11,13,15},{16,18,20,22,24,26,28,30},{17..., dimensions={0} | all-to-all | bytes 524288 | tf_op jit(solution)/shard_map/projection_sum/all_to_all | solution.py:94
  78.8 0.1 copy.15
  78.9 0.4 fusion.8
  79.3 13.5 %all_to_all.70 = f32[32,8,256]{2,1,0:T(8,128)S(1)} all-to-all(f32[32,8,256]{2,1,0:T(8,128)S(1)} %fusion.8), channel_id=1, replica_groups=mesh['row'=32,'col'=16] {'row'}, dimensions={0} | all-to-all | bytes 524288 | tf_op jit(solution)/shard_map/gram_sum/all_to_all | solution.py:94
  92.9 14.0 %all_to_all.71 = f32[32,8,256]{2,1,0:T(8,128)S(1)} all-to-all(f32[32,8,256]{2,1,0:T(8,128)S(1)} %broadcast_in_dim.28), channel_id=1, replica_groups=mesh['row'=32,'col'=16] {'row'}, dimensions={0} | all-to-all | bytes 524288 | tf_op jit(solution)/shard_map/gram_sum/all_to_all | solution.py:94
  106.9 7.6 %whiten.1 = bf16[256,256]{1,0:T(8,128)(2,1)S(1)} custom-call(f32[256,256]{1,0:T(8,128)S(1)} %bitcast.38, f32[256,256]{1,0:T(8,128)S(1)} %bitcast.37), custom_call_target="tpu_custom_call" | custom-call | tf_op jit(solution)/shard_map/whiten/pallas_call | solution.py:83
  114.5 9.4 %all_to_all.72 = bf16[2,256,256]{2,1,0:T(8,128)(2,1)S(1)} all-to-all(bf16[2,256,256]{2,1,0:T(8,128)(2,1)S(1)} %broadcast_in_dim.29), channel_id=1, replica_groups={{0,1},{2,3},{4,5},{6,7},{8,9},{10,11},{12,13},{14,15},{16,17},{18,19},{..., dimensions={0} | all-to-all | bytes 524288 | tf_op jit(solution)/shard_map/whiten/all_to_all | solution.py:94
  124.0 0.0 copy-start.5
  124.0 0.0 copy-start.6
  124.0 0.3 convolution_convert_fusion.1
  124.4 0.4 convolution_convert_fusion
  124.7 0.1 pad_maximum_fusion
  124.8 17.7 %all_to_all.73 = bf16[4,64,2176]{2,1,0:T(8,128)(2,1)S(1)} all-to-all(bf16[4,64,2176]{2,1,0:T(8,128)(2,1)S(1)} %bitcast.41), channel_id=1, replica_groups={{0,128,256,384},{16,144,272,400},{32,160,288,416},{48,176,304,432},{64,..., dimensions={0} | all-to-all | bytes 2228224 | tf_op jit(solution)/shard_map/coefficients/all_to_all | solution.py:94
  142.5 0.2 reduce_sum.78
  142.7 12.8 %all_to_all.74 = bf16[8,8,2176]{2,1,0:T(8,128)(2,1)S(1)} all-to-all(bf16[8,8,2176]{2,1,0:T(8,128)(2,1)S(1)} %bitcast.44), channel_id=1, replica_groups={{0,16,32,48,64,80,96,112},{128,144,160,176,192,208,224,240},{256,272,28..., dimensions={0} | all-to-all | bytes 557056 | tf_op jit(solution)/shard_map/coefficients/all_to_all | solution.py:94
  155.6 0.1 slice_reduce_fusion.1
  155.7 0.1 slice_reduce_fusion
  155.9 0.1 broadcast_in_dim.30
  155.9 0.1 broadcast_in_dim.31
  156.0 0.1 pad_maximum_fusion.3
  156.1 13.6 %all_to_all.75 = f32[16,8,128]{2,1,0:T(8,128)S(1)} all-to-all(f32[16,8,128]{2,1,0:T(8,128)S(1)} %broadcast_in_dim.32), channel_id=1, replica_groups=mesh['row'=32,'col'=16] {'col'}, dimensions={0} | all-to-all | bytes 131072 | tf_op jit(solution)/shard_map/squares/all_to_all | solution.py:94
  169.7 0.2 sqrt_reduce_fusion
  169.9 0.7 fusion.13
  170.6 0.7 fusion.12
  171.3 15.0 %all_to_all.76 = bf16[8,8,2176]{2,1,0:T(8,128)(2,1)S(1)} all-to-all(bf16[8,8,2176]{2,1,0:T(8,128)(2,1)S(1)} %broadcast_in_dim.33), channel_id=1, replica_groups={{0,16,32,48,64,80,96,112},{128,144,160,176,192,208,224,240},{256,272,28..., dimensions={0} | all-to-all | bytes 557056 | tf_op jit(solution)/shard_map/coefficient_gather/all_to_all | solution.py:94
  186.3 0.1 broadcast_in_dim.35
  186.4 17.7 %all_to_all.77 = bf16[4,64,2176]{2,1,0:T(8,128)(2,1)S(1)} all-to-all(bf16[4,64,2176]{2,1,0:T(8,128)(2,1)S(1)} %broadcast_in_dim.35), channel_id=1, replica_groups={{0,128,256,384},{16,144,272,400},{32,160,288,416},{48,176,304,432},{64,..., dimensions={0} | all-to-all | bytes 2228224 | tf_op jit(solution)/shard_map/coefficient_gather/all_to_all | solution.py:94
  204.1 0.0 copy-done.5
  204.1 0.0 copy-start.4
  204.1 1.1 fusion.3
  205.2 0.0 copy-done.6
  205.2 0.0 copy-done.4
  205.2 1.2 fusion.1
  (14 shorter events, 0.3 us)
Async XLA Ops:
  22.8 16.9 %copy-start = (bf16[256,1024]{1,0:T(8,128)(2,1)S(1)}, bf16[256,1024]{1,0:T(8,128)(2,1)}, u32[]{:S(2)}) copy-start(bf16[256,1024]{1,0:T(8,128)(2,1)} %param.9) | copy-start | bytes 1572868
  22.8 16.9 %copy-start.1 = (bf16[256,1024]{1,0:T(8,128)(2,1)S(1)}, bf16[256,1024]{1,0:T(8,128)(2,1)}, u32[]{:S(2)}) copy-start(bf16[256,1024]{1,0:T(8,128)(2,1)} %param.10) | copy-start | bytes 1572868
  39.7 1.1 copy-start.2
  39.7 1.2 copy-start.3
  124.0 80.1 %copy-start.5 = (bf16[256,256]{1,0:T(8,128)(2,1)}, bf16[256,256]{1,0:T(8,128)(2,1)S(1)}, u32[]{:S(2)}) copy-start(bf16[256,256]{1,0:T(8,128)(2,1)S(1)} %get-tuple-element.14) | copy-start | bytes 393220
  124.0 81.2 %copy-start.6 = (bf16[256,256]{1,0:T(8,128)(2,1)}, bf16[256,256]{1,0:T(8,128)(2,1)S(1)}, u32[]{:S(2)}) copy-start(bf16[256,256]{1,0:T(8,128)(2,1)S(1)} %get-tuple-element.15) | copy-start | bytes 393220
  204.1 1.1 copy-start.4

commit v3 on v2

--- a/solution.py
+++ b/solution.py
@@ -102,6 +102,50 @@
     return jnp.sum(exchange(blocks, axis, groups).astype(jnp.float32), axis=0)
 
 
+def finish_kernel(scale, count, *refs):
+    moments, grads, lefts, blocks = refs[0:2], refs[2:4], refs[4:6], refs[6 : 6 + count]
+    nexts, low_ref = refs[6 + count : 8 + count], refs[8 + count]
+    depth = blocks[0].shape[0]
+    for at, block in enumerate(blocks):
+        low_ref[at * depth : (at + 1) * depth, :] = block[...]
+    base = 0
+    for moment, grad, left, result in zip(moments, grads, lefts, nexts):
+        wide = moment.shape[1]
+        tile = next(size for size in (512, 384, 256, 128, wide) if wide % size == 0)
+        for at in range(0, wide, tile):
+            feedback = jnp.dot(
+                left[...],
+                low_ref[:, base + at : base + at + tile],
+                preferred_element_type=jnp.float32,
+            )
+            combined = combine_terms(moment[:, at : at + tile], grad[:, at : at + tile])
+            result[:, at : at + tile] = (
+                combined.astype(jnp.float32) - scale * feedback
+            ).astype(jnp.bfloat16)
+        base += wide
+
+
+def finish(moments, grads, lefts, blocks, row_total):
+    rank = lefts[0].shape[1]
+    width = blocks[0].shape[1]
+    rows = moments[0].shape[0]
+    return pl.pallas_call(
+        functools.partial(
+            finish_kernel, (1.0 - MOMENTUM_DECAY) / row_total, len(blocks)
+        ),
+        out_shape=[jax.ShapeDtypeStruct(moment.shape, jnp.bfloat16) for moment in moments],
+        in_specs=[pl.BlockSpec(memory_space=pltpu.VMEM)] * (6 + len(blocks)),
+        out_specs=[pl.BlockSpec(memory_space=pltpu.VMEM)] * 2,
+        scratch_shapes=[pltpu.VMEM((rank, width), jnp.bfloat16)],
+        compiler_params=pltpu.CompilerParams(vmem_limit_bytes=32 * 2**20),
+        cost_estimate=pl.CostEstimate(
+            flops=2 * rows * rank * width,
+            bytes_accessed=8 * rows * width,
+            transcendentals=0,
+        ),
+    )(*moments, *grads, *lefts, *blocks)
+
+
 def per_device(qkv_grad, qkv_moment, qkv_basis, out_grad, out_moment, out_basis):
     row_count = lax.axis_size("row")
     col_count = lax.axis_size("col")
@@ -155,7 +199,7 @@
         gram = gather(gram, "row", row_count).reshape(rank, rank)
     with jax.named_scope("whiten"):
         left = whiten(gram, projection, row_total)
-        left = gather(left, "col", CORES, same_chip)
+        left = lax.all_gather(left, "col", axis_index_groups=same_chip)
     qkv_left, out_left = left[0], left[1]
     with jax.named_scope("coefficients"):
         terms = [
@@ -167,7 +211,29 @@
         terms = jnp.concatenate(terms, axis=1).reshape(outer, DEPTH * share, width)
         terms = scatter_sum(terms, "row", along_x).astype(jnp.bfloat16)
         coeff = scatter_sum(terms.reshape(DEPTH, share, width), "row", along_z)
+    with jax.named_scope("coefficient_gather_z"):
+        low = gather(coeff.astype(jnp.bfloat16), "row", DEPTH, along_z)
+        low = low.reshape(DEPTH * share, width)
+    with jax.named_scope("coefficient_gather_x"):
+        blocks = [low] + [
+            lax.ppermute(
+                low,
+                "row",
+                [
+                    (x * DEPTH + z, (x - step) % outer * DEPTH + z)
+                    for x in range(outer)
+                    for z in range(DEPTH)
+                ],
+            )
+            for step in range(1, outer)
+        ]
+        turn = lax.axis_index("row") // DEPTH * (DEPTH * share)
+        turned = [
+            lax.dynamic_slice_in_dim(jnp.concatenate([part, part], axis=1), turn, rank, 1)
+            for part in (qkv_left, out_left)
+        ]
     with jax.named_scope("squares"):
+        blocks[1], coeff = lax.optimization_barrier((blocks[1], coeff))
         squared = coeff * coeff
         squares = jnp.concatenate(
             [
@@ -181,25 +247,10 @@
         out_scale = jnp.sqrt(squares[:, LANES // 2 : LANES // 2 + 1] / out_total + EPSILON)
         qkv_right = (coeff[:, :qkv_width] / qkv_scale).astype(jnp.bfloat16).T
         out_right = (coeff[:, qkv_width:] / out_scale).astype(jnp.bfloat16).T
-    with jax.named_scope("coefficient_gather"):
-        low, qkv_right, out_right = lax.optimization_barrier(
-            (coeff.astype(jnp.bfloat16), qkv_right, out_right)
+    with jax.named_scope("moment_next"):
+        nexts = finish(
+            (qkv_moment, out_moment), (qkv_grad, out_grad), turned, blocks, row_total
         )
-        low = gather(low, "row", DEPTH, along_z).reshape(DEPTH * share, width)
-        low = gather(low, "row", outer, along_x).reshape(rank, width)
-    with jax.named_scope("moment_next"):
-        nexts = [
-            (
-                combined.astype(jnp.float32)
-                - (1.0 - MOMENTUM_DECAY)
-                / row_total
-                * jnp.dot(part, part_low, preferred_element_type=jnp.float32)
-            ).astype(jnp.bfloat16)
-            for combined, part, part_low in (
-                (qkv_combined, qkv_left, low[:, :qkv_width]),
-                (out_combined, out_left, low[:, qkv_width:]),
-            )
-        ]
     return (nexts[0], qkv_left, qkv_right, nexts[1], out_left, out_right)
 
 

time: 207 us -> 199 us (0.961); the launches traced: 206 us -> 196 us
  blocking collectives: 189 us -> 154 us
  starting transfers between devices: 0 us -> 17.2 us
  waiting for transfers between devices: 0 us -> 5.12 us
  Pallas kernels: 7.62 us -> 10.1 us
  matrix products: 4.11 us -> 1.82 us
    all_to_all x13 -> x10, blocking collectives: 189 us -> 147 us  [exchange(): return lax.all_to_all(blocks, axis, 0, 0, axis_index_groups=groups)]
    all_to_all x0 -> x1, starting transfers between devices: none -> 9.38 us  [exchange(): return lax.all_to_all(blocks, axis, 0, 0, axis_index_groups=groups)]
    ppermute x0 -> x3, starting transfers between devices: none -> 7.79 us  [per_device(): lax.ppermute(low, 'row', [(x * DEPTH + z, (x - step) % outer * DEPTH + z)...]
    all_gather x0 -> x1, blocking collectives: none -> 7.49 us  [per_device(): left = lax.all_gather(left, 'col', axis_index_groups=same_chip)]
    all_to_all x0 -> x1, waiting for transfers between devices: none -> 5.11 us  [exchange(): return lax.all_to_all(blocks, axis, 0, 0, axis_index_groups=groups)]
    pallas_call x0 -> x1, Pallas kernels: none -> 2.43 us  [finish(): pl.pallas_call(functools.partial(finish_kernel, (1.0 - MOMENTUM_DECAY) /...]
    dot_general x2 -> x0, matrix products: 2.3 us -> none  [per_device(): jnp.dot(part, part_low, preferred_element_type=jnp.float32)]
  transfers between devices with their start and end apart: 0 -> 4, of which waited for: 0 -> 1; matrix products, arithmetic and copies ran while one was open for 0% -> 1% of each run, Pallas kernels for 0% -> 1%
where the time goes in v3:
time: 199 us; the launch traced here: 196 us
  blocking collectives  154 us (77%)
  starting transfers between devices  17.2 us (9%)
  Pallas kernels  10.1 us (5%)
  waiting for transfers between devices  5.12 us (3%)
  other arithmetic  4.09 us (2%)
  local copies, waits for them, and re-layouts  2.24 us (1%)
    all_to_all x10, blocking collectives, exchange(): return lax.all_to_all(blocks, axis, 0, 0, axis_index_groups=groups)  147 us
    all_to_all x1, starting transfers between devices, exchange(): return lax.all_to_all(blocks, axis, 0, 0, axis_index_groups=groups)  9.38 us
    ppermute x3, starting transfers between devices, per_device(): lax.ppermute(low, 'row', [(x * DEPTH + z, (x - step) % outer * DEPTH + z)...  7.79 us
    pallas_call x1, Pallas kernels, whiten(): pl.pallas_call(functools.partial(whiten_kernel, float(row_total)), out_sh...  7.63 us
    all_gather x1, blocking collectives, per_device(): left = lax.all_gather(left, 'col', axis_index_groups=same_chip)  7.49 us
    all_to_all x1, waiting for transfers between devices, exchange(): return lax.all_to_all(blocks, axis, 0, 0, axis_index_groups=groups)  5.11 us
  transfers between devices with their start and end apart: 4, of which 1 were waited for; matrix products, arithmetic and copies ran while one was open for 1% of the time, Pallas kernels for 1%

profile of v3, /device:TPU:1, one launch (start us, length us, event | category | flops | bytes accessed | tf_op | source)
XLA Modules:
  0.0 195.8 jit_solution(18239543643451294130)
XLA Ops:
  0.6 0.7 pad_maximum_fusion.2
  1.4 21.3 %all_to_all.55 = bf16[8,8,2176]{2,1,0:T(8,128)(2,1)S(1)} all-to-all(bf16[8,8,2176]{2,1,0:T(8,128)(2,1)S(1)} %broadcast_in_dim.18), channel_id=1, replica_groups={{0,16,32,48,64,80,96,112},{128,144,160,176,192,208,224,240},{256,272,28..., dimensions={0} | all-to-all | bytes 557056 | tf_op jit(solution)/shard_map/basis_gather/all_to_all | solution.py:94
  22.7 0.1 broadcast_in_dim.20
  22.8 0.0 copy-start
  22.8 0.0 copy-start.1
  22.8 16.9 %all_to_all.56 = bf16[4,64,2176]{2,1,0:T(8,128)(2,1)S(1)} all-to-all(bf16[4,64,2176]{2,1,0:T(8,128)(2,1)S(1)} %broadcast_in_dim.20), channel_id=1, replica_groups={{0,128,256,384},{16,144,272,400},{32,160,288,416},{48,176,304,432},{64,..., dimensions={0} | all-to-all | bytes 2228224 | tf_op jit(solution)/shard_map/basis_gather/all_to_all | solution.py:94
  39.7 0.0 copy-start.2
  39.7 0.0 copy-start.3
  39.7 0.0 copy-done
  39.7 0.0 copy-done.1
  39.7 0.3 convolution_bitcast_fusion
  40.1 0.7 copy-done.2
  40.8 0.2 copy-done.3
  40.9 0.4 convolution_bitcast_fusion.1
  41.4 7.6 %all_to_all.57 = f32[2,256,256]{2,1,0:T(8,128)S(1)} all-to-all(f32[2,256,256]{2,1,0:T(8,128)S(1)} %pad_maximum_fusion.1), channel_id=1, replica_groups={{0,1},{2,3},{4,5},{6,7},{8,9},{10,11},{12,13},{14,15},{16,17},{18,19},{..., dimensions={0} | all-to-all | bytes 1048576 | tf_op jit(solution)/shard_map/projection_sum/all_to_all | solution.py:94
  49.0 17.7 %all_to_all.58 = f32[8,32,256]{2,1,0:T(8,128)S(1)} all-to-all(f32[8,32,256]{2,1,0:T(8,128)S(1)} %bitcast.41), channel_id=1, replica_groups={{0,2,4,6,8,10,12,14},{1,3,5,7,9,11,13,15},{16,18,20,22,24,26,28,30},{17..., dimensions={0} | all-to-all | bytes 524288 | tf_op jit(solution)/shard_map/projection_sum/all_to_all | solution.py:94
  66.7 12.1 %all_to_all.59 = f32[8,32,256]{2,1,0:T(8,128)S(1)} all-to-all(f32[8,32,256]{2,1,0:T(8,128)S(1)} %broadcast_in_dim.21), channel_id=1, replica_groups={{0,2,4,6,8,10,12,14},{1,3,5,7,9,11,13,15},{16,18,20,22,24,26,28,30},{17..., dimensions={0} | all-to-all | bytes 524288 | tf_op jit(solution)/shard_map/projection_sum/all_to_all | solution.py:94
  78.8 0.1 copy.15
  78.9 0.4 fusion.2
  79.3 13.5 %all_to_all.60 = f32[32,8,256]{2,1,0:T(8,128)S(1)} all-to-all(f32[32,8,256]{2,1,0:T(8,128)S(1)} %fusion.2), channel_id=1, replica_groups=mesh['row'=32,'col'=16] {'row'}, dimensions={0} | all-to-all | bytes 524288 | tf_op jit(solution)/shard_map/gram_sum/all_to_all | solution.py:94
  92.9 14.0 %all_to_all.61 = f32[32,8,256]{2,1,0:T(8,128)S(1)} all-to-all(f32[32,8,256]{2,1,0:T(8,128)S(1)} %broadcast_in_dim.22), channel_id=1, replica_groups=mesh['row'=32,'col'=16] {'row'}, dimensions={0} | all-to-all | bytes 524288 | tf_op jit(solution)/shard_map/gram_sum/all_to_all | solution.py:94
  106.9 7.6 %whiten.1 = bf16[256,256]{1,0:T(8,128)(2,1)S(1)} custom-call(f32[256,256]{1,0:T(8,128)S(1)} %bitcast.35, f32[256,256]{1,0:T(8,128)S(1)} %bitcast.30), custom_call_target="tpu_custom_call" | custom-call | tf_op jit(solution)/shard_map/whiten/pallas_call | solution.py:83
  114.5 7.5 %all-gather = bf16[512,256]{1,0:T(8,128)(2,1)S(1)} all-gather(bf16[256,256]{1,0:T(8,128)(2,1)S(1)} %whiten.1), channel_id=2, replica_groups={{0,1},{2,3},{4,5},{6,7},{8,9},{10,11},{12,13},{14,15},{16,17},{18,19},{..., dimensions={0}, use_global_device_ids=true | all-gather | bytes 393216 | tf_op jit(solution)/shard_map/whiten/all_gather | solution.py:202
  122.0 0.0 copy-start.5
  122.0 0.0 copy-start.4
  122.1 0.4 convolution_convert_fusion
  122.4 0.3 copy-done.5
  122.7 0.3 convolution_convert_fusion.1
  123.0 0.1 pad_maximum_fusion
  123.1 17.7 %all_to_all.62 = bf16[4,64,2176]{2,1,0:T(8,128)(2,1)S(1)} all-to-all(bf16[4,64,2176]{2,1,0:T(8,128)(2,1)S(1)} %bitcast.36), channel_id=1, replica_groups={{0,128,256,384},{16,144,272,400},{32,160,288,416},{48,176,304,432},{64,..., dimensions={0} | all-to-all | bytes 2228224 | tf_op jit(solution)/shard_map/coefficients/all_to_all | solution.py:94
  140.8 0.9 reduce_sum.78
  141.7 0.0 copy-start.6
  141.7 13.6 %all_to_all.63 = bf16[8,8,2176]{2,1,0:T(8,128)(2,1)S(1)} all-to-all(bf16[8,8,2176]{2,1,0:T(8,128)(2,1)} %bitcast.39), channel_id=1, replica_groups={{0,16,32,48,64,80,96,112},{128,144,160,176,192,208,224,240},{256,272,28..., dimensions={0} | all-to-all | bytes 557056 | tf_op jit(solution)/shard_map/coefficients/all_to_all | solution.py:94
  155.5 12.6 %all_to_all.64 = bf16[8,8,2176]{2,1,0:T(8,128)(2,1)S(1)} all-to-all(bf16[8,8,2176]{2,1,0:T(8,128)(2,1)S(1)} %broadcast_in_dim.23), channel_id=1, replica_groups={{0,16,32,48,64,80,96,112},{128,144,160,176,192,208,224,240},{256,272,28..., dimensions={0} | all-to-all | bytes 557056 | tf_op jit(solution)/shard_map/coefficient_gather_z/all_to_all | solution.py:94
  168.0 2.8 %collective-permute-start = (bf16[64,2176]{1,0:T(8,128)(2,1)S(1)}, bf16[64,2176]{1,0:T(8,128)(2,1)S(1)}, u32[]{:S(2)}, u32[]{:S(2)}) collective-permute-start(bf16[64,2176]{1,0:T(8,128)(2,1)S(1)} %bitcast.31), channel_id=1, source_target_pairs={{0,384},{16,400},{32,416},{48,432},{64,448},{80,464},{96,480},{112... | collective-permute-start | bytes 835592 | tf_op jit(solution)/shard_map/coefficient_gather_x/ppermute | solution.py:219
  170.8 3.1 %collective-permute-start.1 = (bf16[64,2176]{1,0:T(8,128)(2,1)S(1)}, bf16[64,2176]{1,0:T(8,128)(2,1)S(1)}, u32[]{:S(2)}, u32[]{:S(2)}) collective-permute-start(bf16[64,2176]{1,0:T(8,128)(2,1)S(1)} %bitcast.32), channel_id=1, source_target_pairs={{0,256},{16,272},{32,288},{48,304},{64,320},{80,336},{96,352},{112... | collective-permute-start | bytes 835592 | tf_op jit(solution)/shard_map/coefficient_gather_x/ppermute | solution.py:219
  173.9 1.9 collective-permute-start.2
  175.9 0.0 collective-permute-done.refs_7_
  175.9 0.1 slice_reduce_fusion
  176.0 0.1 slice_reduce_fusion.1
  176.1 0.1 broadcast_in_dim.24
  176.2 0.1 broadcast_in_dim.25
  176.3 0.1 pad_maximum_fusion.3
  176.3 0.6 broadcast_in_dim.26
  177.0 9.4 %all-to-all-start.10 = ((f32[16,8,128]{2,1,0:T(8,128)}), f32[16,8,128]{2,1,0:T(8,128)S(1)}, u32[]{:S(2)}, u32[]{:S(2)}) async-start(f32[16,8,128]{2,1,0:T(8,128)} %broadcast_in_dim.26), calls=%async_computation.10 | async-start | bytes 131072 | tf_op jit(solution)/shard_map/squares/all_to_all | solution.py:94
  186.4 0.0 copy-done.4
  186.4 0.0 copy-done.6
  186.4 0.3 fusion.4
  186.6 0.0 collective-permute-done.1.refs_8_
  186.6 0.0 collective-permute-done.2.refs_9_
  186.6 2.4 %moment_next.1 = (bf16[256,1152]{1,0:T(8,128)(2,1)}, bf16[256,1024]{1,0:T(8,128)(2,1)}) custom-call(bf16[256,1152]{1,0:T(8,128)(2,1)S(1)} %copy-done.2, bf16[256,1024]{1,0:T(8,128)(2,1)S(1)} %copy-done, bf16[256,1152]{1,0:T(8,128)(2,1)S(1)} %copy-done.3, bf16[256,1024]{1,0:T(8,128)(2,1)S(1)} %copy-done.1, bf16[256,256]{1,0:T(8,128)(2,1)S(1)} %get-tuple-element.19.refs_4_, ...), custom_call_target="tpu_custom_call" | custom-call | flops 285212672 | bytes 4456448 | tf_op jit(solution)/shard_map/moment_next/pallas_call | solution.py:132
  189.1 5.1 %all-to-all-done.10 = f32[16,8,128]{2,1,0:T(8,128)S(1)} async-done(((f32[16,8,128]{2,1,0:T(8,128)}), f32[16,8,128]{2,1,0:T(8,128)S(1)}, u32[]{:S(2)}, u32[]{:S(2)}) %all-to-all-start.10) | async-done | bytes 65568 | tf_op jit(solution)/shard_map/squares/all_to_all | solution.py:94
  194.2 0.2 sqrt_reduce_fusion
  194.4 0.7 fusion.7
  195.1 0.7 fusion.6
  (13 shorter events, 0.3 us)
Async XLA Ops:
  22.8 16.9 %copy-start = (bf16[256,1024]{1,0:T(8,128)(2,1)S(1)}, bf16[256,1024]{1,0:T(8,128)(2,1)}, u32[]{:S(2)}) copy-start(bf16[256,1024]{1,0:T(8,128)(2,1)} %refs_1_.1) | copy-start | bytes 1572868
  22.8 16.9 %copy-start.1 = (bf16[256,1024]{1,0:T(8,128)(2,1)S(1)}, bf16[256,1024]{1,0:T(8,128)(2,1)}, u32[]{:S(2)}) copy-start(bf16[256,1024]{1,0:T(8,128)(2,1)} %refs_3_.1) | copy-start | bytes 1572868
  39.7 1.1 copy-start.2
  39.7 1.2 copy-start.3
  122.0 0.7 copy-start.5
  122.0 64.3 %copy-start.4 = (bf16[256,256]{1,0:T(8,128)(2,1)}, bf16[256,256]{1,0:T(8,128)(2,1)S(1)}, u32[]{:S(2)}) copy-start(bf16[256,256]{1,0:T(8,128)(2,1)S(1)} %get-tuple-element.16) | copy-start | bytes 393220
  141.7 44.6 %copy-start.6 = (bf16[256,256]{1,0:T(8,128)(2,1)S(1)}, bf16[256,256]{1,0:T(8,128)(2,1)}, u32[]{:S(2)}) copy-start(bf16[256,256]{1,0:T(8,128)(2,1)} %copy-done.5) | copy-start | bytes 393220
  168.0 7.8 %collective-permute-start = (bf16[64,2176]{1,0:T(8,128)(2,1)S(1)}, bf16[64,2176]{1,0:T(8,128)(2,1)S(1)}, u32[]{:S(2)}, u32[]{:S(2)}) collective-permute-start(bf16[64,2176]{1,0:T(8,128)(2,1)S(1)} %bitcast.31), channel_id=1, source_target_pairs={{0,384},{16,400},{32,416},{48,432},{64,448},{80,464},{96,480},{112... | collective-permute-start | bytes 835592 | tf_op jit(solution)/shard_map/coefficient_gather_x/ppermute | solution.py:219
  170.8 15.8 %collective-permute-start.1 = (bf16[64,2176]{1,0:T(8,128)(2,1)S(1)}, bf16[64,2176]{1,0:T(8,128)(2,1)S(1)}, u32[]{:S(2)}, u32[]{:S(2)}) collective-permute-start(bf16[64,2176]{1,0:T(8,128)(2,1)S(1)} %bitcast.32), channel_id=1, source_target_pairs={{0,256},{16,272},{32,288},{48,304},{64,320},{80,336},{96,352},{112... | collective-permute-start | bytes 835592 | tf_op jit(solution)/shard_map/coefficient_gather_x/ppermute | solution.py:219
  173.9 12.7 %collective-permute-start.2 = (bf16[64,2176]{1,0:T(8,128)(2,1)S(1)}, bf16[64,2176]{1,0:T(8,128)(2,1)}, u32[]{:S(2)}, u32[]{:S(2)}) collective-permute-start(bf16[64,2176]{1,0:T(8,128)(2,1)S(1)} %bitcast.33), channel_id=1, source_target_pairs={{0,128},{16,144},{32,160},{48,176},{64,192},{80,208},{96,224},{112... | collective-permute-start | bytes 835592 | tf_op jit(solution)/shard_map/coefficient_gather_x/ppermute | solution.py:219
  177.0 17.2 %all-to-all-start.10 = ((f32[16,8,128]{2,1,0:T(8,128)}), f32[16,8,128]{2,1,0:T(8,128)S(1)}, u32[]{:S(2)}, u32[]{:S(2)}) async-start(f32[16,8,128]{2,1,0:T(8,128)} %broadcast_in_dim.26), calls=%async_computation.10 | async-start | bytes 131072 | tf_op jit(solution)/shard_map/squares/all_to_all | solution.py:94

commit v4 on v3

--- a/solution.py
+++ b/solution.py
@@ -29,11 +29,13 @@
     return high, middle, low
 
 
-def whiten_kernel(row_total, gram_ref, proj_ref, left_ref, work_ref):
-    size = gram_ref.shape[0]
+def whiten_kernel(row_total, top_ref, corner_ref, proj_ref, left_ref, work_ref):
+    half, size = top_ref.shape
     rows = proj_ref.shape[0]
     width = size + rows
-    work_ref[:, :size] = gram_ref[...] * (1.0 / row_total)
+    work_ref[:half, :size] = top_ref[...] * (1.0 / row_total)
+    work_ref[half:size, half:size] = corner_ref[...] * (1.0 / row_total)
+    work_ref[half:size, :half] = jnp.zeros((size - half, half), jnp.float32)
     work_ref[:, size:] = proj_ref[...].T
     row = lax.broadcasted_iota(jnp.int32, (PANEL, LANES), 0)
     for start in range(0, size, PANEL):
@@ -77,17 +79,17 @@
     left_ref[...] = work_ref[:, size:].T.astype(left_ref.dtype)
 
 
-def whiten(gram_sum, projection, row_total):
-    size = gram_sum.shape[0]
+def whiten(top, corner, projection, row_total):
+    size = top.shape[1]
     rows = projection.shape[0]
     return pl.pallas_call(
         functools.partial(whiten_kernel, float(row_total)),
         out_shape=jax.ShapeDtypeStruct((rows, size), jnp.bfloat16),
-        in_specs=[pl.BlockSpec(memory_space=pltpu.VMEM)] * 2,
+        in_specs=[pl.BlockSpec(memory_space=pltpu.VMEM)] * 3,
         out_specs=pl.BlockSpec(memory_space=pltpu.VMEM),
         scratch_shapes=[pltpu.VMEM((size, size + rows), jnp.float32)],
         compiler_params=pltpu.CompilerParams(vmem_limit_bytes=32 * 2**20),
-    )(gram_sum, projection)
+    )(top, corner, projection)
 
 
 def exchange(blocks, axis, groups=None):
@@ -182,9 +184,14 @@
                 (out_combined, basis[:, qkv_width:]),
             )
         ]
-        partial = jnp.stack(partial)
     with jax.named_scope("projection_sum"):
-        own = scatter_sum(partial, "col", same_chip)
+        first = lax.axis_index("col") % CORES == 0
+        other = lax.ppermute(
+            jnp.where(first, partial[1], partial[0]),
+            "col",
+            [(source, source ^ 1) for source in range(col_count)],
+        )
+        own = jnp.where(first, partial[0], partial[1]) + other
         own = own.reshape(chips, local_rows // chips, rank)
         own = scatter_sum(own, "col", same_core)
         projection = gather(own, "col", chips, same_core).reshape(local_rows, rank)
@@ -195,10 +202,19 @@
             precision=lax.Precision.HIGHEST,
             preferred_element_type=jnp.float32,
         )
-        gram = scatter_sum(gram.reshape(row_count, share, rank), "row")
-        gram = gather(gram, "row", row_count).reshape(rank, rank)
+        half = rank // 2
+        packed = jnp.concatenate(
+            [
+                gram[:half].reshape(row_count, half // row_count, rank),
+                gram[half:, half:].reshape(row_count, half // row_count, half),
+            ],
+            axis=2,
+        )
+        packed = gather(scatter_sum(packed, "row"), "row", row_count)
+        top = packed[:, :, :rank].reshape(half, rank)
+        corner = packed[:, :, rank:].reshape(half, half)
     with jax.named_scope("whiten"):
-        left = whiten(gram, projection, row_total)
+        left = whiten(top, corner, projection, row_total)
         left = lax.all_gather(left, "col", axis_index_groups=same_chip)
     qkv_left, out_left = left[0], left[1]
     with jax.named_scope("coefficients"):

time: 199 us -> 199 us (level)
  blocking collectives: 154 us -> 129 us
  waiting for transfers between devices: 5.12 us -> 19.1 us
  starting transfers between devices: 17.2 us -> 27.9 us
    all_to_all x10 -> x8, blocking collectives: 147 us -> 122 us  [exchange(): return lax.all_to_all(blocks, axis, 0, 0, axis_index_groups=groups)]
    all_to_all x1 -> x2, waiting for transfers between devices: 5.11 us -> 17.9 us  [exchange(): return lax.all_to_all(blocks, axis, 0, 0, axis_index_groups=groups)]
    ppermute x0 -> x1, starting transfers between devices: none -> 5.99 us  [per_device(): lax.ppermute(jnp.where(first, partial[1], partial[0]), 'col', [(source, s...]
    all_to_all x1 -> x2, starting transfers between devices: 9.38 us -> 14.1 us  [exchange(): return lax.all_to_all(blocks, axis, 0, 0, axis_index_groups=groups)]
  transfers between devices with their start and end apart: 4 -> 6, of which waited for: 1 -> 3; matrix products, arithmetic and copies ran while one was open for 1% -> 1% of each run, Pallas kernels for 1% -> 1%
where the time goes in v4:
time: 199 us; the launch traced here: 196 us
  blocking collectives  129 us (65%)
  starting transfers between devices  27.9 us (14%)
  waiting for transfers between devices  19.1 us (10%)
  Pallas kernels  9.11 us (5%)
  other arithmetic  5.89 us (3%)
  local copies, waits for them, and re-layouts  2.35 us (1%)
  matrix products  2.03 us (1%)
    all_to_all x8, blocking collectives, exchange(): return lax.all_to_all(blocks, axis, 0, 0, axis_index_groups=groups)  122 us
    all_to_all x2, waiting for transfers between devices, exchange(): return lax.all_to_all(blocks, axis, 0, 0, axis_index_groups=groups)  17.9 us
    all_to_all x2, starting transfers between devices, exchange(): return lax.all_to_all(blocks, axis, 0, 0, axis_index_groups=groups)  14.1 us
    ppermute x3, starting transfers between devices, per_device(): lax.ppermute(low, 'row', [(x * DEPTH + z, (x - step) % outer * DEPTH + z)...  7.79 us
    pallas_call x1, Pallas kernels, whiten(): pl.pallas_call(functools.partial(whiten_kernel, float(row_total)), out_sh...  7.63 us
    all_gather x1, blocking collectives, per_device(): left = lax.all_gather(left, 'col', axis_index_groups=same_chip)  7.4 us
    ppermute x1, starting transfers between devices, per_device(): lax.ppermute(jnp.where(first, partial[1], partial[0]), 'col', [(source, s...  5.99 us
  transfers between devices with their start and end apart: 6, of which 3 were waited for; matrix products, arithmetic and copies ran while one was open for 1% of the time, Pallas kernels for 1%

profile of v4, /device:TPU:1, one launch (start us, length us, event | category | flops | bytes accessed | tf_op | source)
XLA Modules:
  0.0 196.2 jit_solution(14979188100599617324)
XLA Ops:
  0.6 0.7 pad_maximum_fusion.2
  1.4 21.3 %all_to_all.50 = bf16[8,8,2176]{2,1,0:T(8,128)(2,1)S(1)} all-to-all(bf16[8,8,2176]{2,1,0:T(8,128)(2,1)S(1)} %broadcast_in_dim.18), channel_id=1, replica_groups={{0,16,32,48,64,80,96,112},{128,144,160,176,192,208,224,240},{256,272,28..., dimensions={0} | all-to-all | bytes 557056 | tf_op jit(solution)/shard_map/basis_gather/all_to_all | solution.py:96
  22.7 1.1 broadcast_in_dim.20
  23.7 0.0 copy-start.2
  23.7 0.0 copy-start.3
  23.7 4.1 %all-to-all-start.1 = ((bf16[4,64,2176]{2,1,0:T(8,128)(2,1)}), bf16[4,64,2176]{2,1,0:T(8,128)(2,1)S(1)}, u32[]{:S(2)}, u32[]{:S(2)}) async-start(bf16[4,64,2176]{2,1,0:T(8,128)(2,1)} %broadcast_in_dim.20), calls=%async_computation.1 | async-start | bytes 2228224 | tf_op jit(solution)/shard_map/basis_gather/all_to_all | solution.py:96
  27.9 0.0 copy-start
  27.9 0.0 copy-start.1
  27.9 12.7 %all-to-all-done.1 = bf16[4,64,2176]{2,1,0:T(8,128)(2,1)S(1)} async-done(((bf16[4,64,2176]{2,1,0:T(8,128)(2,1)}), bf16[4,64,2176]{2,1,0:T(8,128)(2,1)S(1)}, u32[]{:S(2)}, u32[]{:S(2)}) %all-to-all-start.1) | async-done | bytes 1114144 | tf_op jit(solution)/shard_map/basis_gather/all_to_all | solution.py:96
  40.6 0.0 copy-done.2
  40.6 0.0 copy-done.3
  40.6 0.4 fusion
  41.0 0.0 copy-done
  41.0 0.0 copy-done.1
  41.0 0.3 broadcast_select_fusion
  41.3 6.0 %collective-permute-start = (f32[256,256]{1,0:T(8,128)S(1)}, f32[256,256]{1,0:T(8,128)S(1)}, u32[]{:S(2)}, u32[]{:S(2)}) collective-permute-start(f32[256,256]{1,0:T(8,128)S(1)} %get-tuple-element.18), channel_id=1, source_target_pairs={{0,1},{1,0},{2,3},{3,2},{4,5},{5,4},{6,7},{7,6},{8,9},{9,8},{10,11... | collective-permute-start | bytes 786440 | tf_op jit(solution)/shard_map/projection_sum/ppermute | solution.py:189
  47.3 1.1 collective-permute-done
  48.5 0.1 select_add_fusion
  48.5 17.7 %all_to_all.51 = f32[8,32,256]{2,1,0:T(8,128)S(1)} all-to-all(f32[8,32,256]{2,1,0:T(8,128)S(1)} %bitcast.32), channel_id=1, replica_groups={{0,2,4,6,8,10,12,14},{1,3,5,7,9,11,13,15},{16,18,20,22,24,26,28,30},{17..., dimensions={0} | all-to-all | bytes 524288 | tf_op jit(solution)/shard_map/projection_sum/all_to_all | solution.py:96
  66.3 12.1 %all_to_all.52 = f32[8,32,256]{2,1,0:T(8,128)S(1)} all-to-all(f32[8,32,256]{2,1,0:T(8,128)S(1)} %broadcast_in_dim.21), channel_id=1, replica_groups={{0,2,4,6,8,10,12,14},{1,3,5,7,9,11,13,15},{16,18,20,22,24,26,28,30},{17..., dimensions={0} | all-to-all | bytes 524288 | tf_op jit(solution)/shard_map/projection_sum/all_to_all | solution.py:96
  78.3 0.6 convolution_bitcast_fusion
  79.1 13.2 %all_to_all.53 = f32[32,4,384]{2,1,0:T(4,128)S(1)} all-to-all(f32[32,4,384]{2,1,0:T(4,128)S(1)} %pad_maximum_fusion.1), channel_id=1, replica_groups=mesh['row'=32,'col'=16] {'row'}, dimensions={0} | all-to-all | bytes 393216 | tf_op jit(solution)/shard_map/gram_sum/all_to_all | solution.py:96
  92.3 0.1 reduce_sum.67
  92.4 13.4 %all_to_all.54 = f32[32,4,384]{2,1,0:T(4,128)S(1)} all-to-all(f32[32,4,384]{2,1,0:T(4,128)S(1)} %broadcast_in_dim.22), channel_id=1, replica_groups=mesh['row'=32,'col'=16] {'row'}, dimensions={0} | all-to-all | bytes 393216 | tf_op jit(solution)/shard_map/gram_sum/all_to_all | solution.py:96
  105.9 7.6 %whiten.1 = bf16[256,256]{1,0:T(8,128)(2,1)S(1)} custom-call(f32[128,256]{1,0:T(8,128)S(1)} %reshape.57.top_ref, f32[128,128]{1,0:T(8,128)S(1)} %bitcast.26, f32[256,256]{1,0:T(8,128)S(1)} %bitcast.25), custom_call_target="tpu_custom_call" | custom-call | tf_op jit(solution)/shard_map/whiten/pallas_call | solution.py:85
  113.5 7.4 %all-gather = bf16[512,256]{1,0:T(8,128)(2,1)S(1)} all-gather(bf16[256,256]{1,0:T(8,128)(2,1)S(1)} %whiten.1), channel_id=2, replica_groups={{0,1},{2,3},{4,5},{6,7},{8,9},{10,11},{12,13},{14,15},{16,17},{18,19},{..., dimensions={0}, use_global_device_ids=true | all-gather | bytes 393216 | tf_op jit(solution)/shard_map/whiten/all_gather | solution.py:218
  121.0 0.0 copy-start.5
  121.0 0.0 copy-start.4
  121.0 0.4 convolution_convert_fusion
  121.4 0.3 copy-done.5
  121.6 0.3 convolution_convert_fusion.1
  122.0 0.1 pad_maximum_fusion
  122.1 17.7 %all_to_all.55 = bf16[4,64,2176]{2,1,0:T(8,128)(2,1)S(1)} all-to-all(bf16[4,64,2176]{2,1,0:T(8,128)(2,1)S(1)} %bitcast.27), channel_id=1, replica_groups={{0,128,256,384},{16,144,272,400},{32,160,288,416},{48,176,304,432},{64,..., dimensions={0} | all-to-all | bytes 2228224 | tf_op jit(solution)/shard_map/coefficients/all_to_all | solution.py:96
  139.8 0.9 reduce_sum.68
  140.7 13.6 %all_to_all.56 = bf16[8,8,2176]{2,1,0:T(8,128)(2,1)S(1)} all-to-all(bf16[8,8,2176]{2,1,0:T(8,128)(2,1)} %bitcast.30), channel_id=1, replica_groups={{0,16,32,48,64,80,96,112},{128,144,160,176,192,208,224,240},{256,272,28..., dimensions={0} | all-to-all | bytes 557056 | tf_op jit(solution)/shard_map/coefficients/all_to_all | solution.py:96
  154.4 12.5 %all_to_all.57 = bf16[8,8,2176]{2,1,0:T(8,128)(2,1)S(1)} all-to-all(bf16[8,8,2176]{2,1,0:T(8,128)(2,1)S(1)} %broadcast_in_dim.23), channel_id=1, replica_groups={{0,16,32,48,64,80,96,112},{128,144,160,176,192,208,224,240},{256,272,28..., dimensions={0} | all-to-all | bytes 557056 | tf_op jit(solution)/shard_map/coefficient_gather_z/all_to_all | solution.py:96
  166.9 2.8 %collective-permute-start.1 = (bf16[64,2176]{1,0:T(8,128)(2,1)S(1)}, bf16[64,2176]{1,0:T(8,128)(2,1)S(1)}, u32[]{:S(2)}, u32[]{:S(2)}) collective-permute-start(bf16[64,2176]{1,0:T(8,128)(2,1)S(1)} %bitcast.21), channel_id=1, source_target_pairs={{0,384},{16,400},{32,416},{48,432},{64,448},{80,464},{96,480},{112... | collective-permute-start | bytes 835592 | tf_op jit(solution)/shard_map/coefficient_gather_x/ppermute | solution.py:235
  169.7 3.1 %collective-permute-start.2 = (bf16[64,2176]{1,0:T(8,128)(2,1)S(1)}, bf16[64,2176]{1,0:T(8,128)(2,1)S(1)}, u32[]{:S(2)}, u32[]{:S(2)}) collective-permute-start(bf16[64,2176]{1,0:T(8,128)(2,1)S(1)} %bitcast.22), channel_id=1, source_target_pairs={{0,256},{16,272},{32,288},{48,304},{64,320},{80,336},{96,352},{112... | collective-permute-start | bytes 835592 | tf_op jit(solution)/shard_map/coefficient_gather_x/ppermute | solution.py:235
  172.8 1.9 collective-permute-start.3
  174.7 0.0 collective-permute-done.1.refs_7_
  174.8 0.1 slice_reduce_fusion
  174.9 0.1 slice_reduce_fusion.1
  175.0 0.1 broadcast_in_dim.24
  175.1 0.1 broadcast_in_dim.25
  175.1 0.1 pad_maximum_fusion.3
  175.2 0.6 broadcast_in_dim.26
  175.8 10.0 %all-to-all-start.9 = ((f32[16,8,128]{2,1,0:T(8,128)}), f32[16,8,128]{2,1,0:T(8,128)}, u32[]{:S(2)}, u32[]{:S(2)}) async-start(f32[16,8,128]{2,1,0:T(8,128)} %broadcast_in_dim.26), calls=%async_computation.9 | async-start | bytes 131072 | tf_op jit(solution)/shard_map/squares/all_to_all | solution.py:96
  185.8 0.0 copy-done.4
  185.8 1.2 fusion.4
  187.0 0.0 collective-permute-done.2.refs_8_
  187.0 0.0 collective-permute-done.3.refs_9_
  187.0 1.5 moment_next.1
  188.5 5.3 %all-to-all-done.9 = f32[16,8,128]{2,1,0:T(8,128)} async-done(((f32[16,8,128]{2,1,0:T(8,128)}), f32[16,8,128]{2,1,0:T(8,128)}, u32[]{:S(2)}, u32[]{:S(2)}) %all-to-all-start.9) | async-done | bytes 65568 | tf_op jit(solution)/shard_map/squares/all_to_all | solution.py:96
  193.7 0.9 reduce_sum.72
  194.6 0.2 sqrt_reduce_fusion
  194.8 0.7 fusion.7
  195.5 0.7 fusion.6
  (16 shorter events, 0.4 us)
Async XLA Ops:
  23.7 16.8 %copy-start.2 = (bf16[256,1152]{1,0:T(8,128)(2,1)S(1)}, bf16[256,1152]{1,0:T(8,128)(2,1)}, u32[]{:S(2)}) copy-start(bf16[256,1152]{1,0:T(8,128)(2,1)} %refs_0_.1) | copy-start | bytes 1769476
  23.7 16.8 %copy-start.3 = (bf16[256,1152]{1,0:T(8,128)(2,1)S(1)}, bf16[256,1152]{1,0:T(8,128)(2,1)}, u32[]{:S(2)}) copy-start(bf16[256,1152]{1,0:T(8,128)(2,1)} %refs_2_.1) | copy-start | bytes 1769476
  23.7 16.8 %all-to-all-start.1 = ((bf16[4,64,2176]{2,1,0:T(8,128)(2,1)}), bf16[4,64,2176]{2,1,0:T(8,128)(2,1)S(1)}, u32[]{:S(2)}, u32[]{:S(2)}) async-start(bf16[4,64,2176]{2,1,0:T(8,128)(2,1)} %broadcast_in_dim.20), calls=%async_computation.1 | async-start | bytes 2228224 | tf_op jit(solution)/shard_map/basis_gather/all_to_all | solution.py:96
  27.9 13.1 %copy-start = (bf16[256,1024]{1,0:T(8,128)(2,1)S(1)}, bf16[256,1024]{1,0:T(8,128)(2,1)}, u32[]{:S(2)}) copy-start(bf16[256,1024]{1,0:T(8,128)(2,1)} %refs_1_.1) | copy-start | bytes 1572868
  27.9 13.1 %copy-start.1 = (bf16[256,1024]{1,0:T(8,128)(2,1)S(1)}, bf16[256,1024]{1,0:T(8,128)(2,1)}, u32[]{:S(2)}) copy-start(bf16[256,1024]{1,0:T(8,128)(2,1)} %refs_3_.1) | copy-start | bytes 1572868
  41.3 7.1 %collective-permute-start = (f32[256,256]{1,0:T(8,128)S(1)}, f32[256,256]{1,0:T(8,128)S(1)}, u32[]{:S(2)}, u32[]{:S(2)}) collective-permute-start(f32[256,256]{1,0:T(8,128)S(1)} %get-tuple-element.18), channel_id=1, source_target_pairs={{0,1},{1,0},{2,3},{3,2},{4,5},{5,4},{6,7},{7,6},{8,9},{9,8},{10,11... | collective-permute-start | bytes 786440 | tf_op jit(solution)/shard_map/projection_sum/ppermute | solution.py:189
  121.0 0.7 copy-start.5
  121.0 64.8 %copy-start.4 = (bf16[256,256]{1,0:T(8,128)(2,1)}, bf16[256,256]{1,0:T(8,128)(2,1)S(1)}, u32[]{:S(2)}) copy-start(bf16[256,256]{1,0:T(8,128)(2,1)S(1)} %get-tuple-element.16) | copy-start | bytes 393220
  166.9 7.8 %collective-permute-start.1 = (bf16[64,2176]{1,0:T(8,128)(2,1)S(1)}, bf16[64,2176]{1,0:T(8,128)(2,1)S(1)}, u32[]{:S(2)}, u32[]{:S(2)}) collective-permute-start(bf16[64,2176]{1,0:T(8,128)(2,1)S(1)} %bitcast.21), channel_id=1, source_target_pairs={{0,384},{16,400},{32,416},{48,432},{64,448},{80,464},{96,480},{112... | collective-permute-start | bytes 835592 | tf_op jit(solution)/shard_map/coefficient_gather_x/ppermute | solution.py:235
  169.7 17.3 %collective-permute-start.2 = (bf16[64,2176]{1,0:T(8,128)(2,1)S(1)}, bf16[64,2176]{1,0:T(8,128)(2,1)S(1)}, u32[]{:S(2)}, u32[]{:S(2)}) collective-permute-start(bf16[64,2176]{1,0:T(8,128)(2,1)S(1)} %bitcast.22), channel_id=1, source_target_pairs={{0,256},{16,272},{32,288},{48,304},{64,320},{80,336},{96,352},{112... | collective-permute-start | bytes 835592 | tf_op jit(solution)/shard_map/coefficient_gather_x/ppermute | solution.py:235
  172.8 14.2 %collective-permute-start.3 = (bf16[64,2176]{1,0:T(8,128)(2,1)S(1)}, bf16[64,2176]{1,0:T(8,128)(2,1)S(1)}, u32[]{:S(2)}, u32[]{:S(2)}) collective-permute-start(bf16[64,2176]{1,0:T(8,128)(2,1)S(1)} %bitcast.23), channel_id=1, source_target_pairs={{0,128},{16,144},{32,160},{48,176},{64,192},{80,208},{96,224},{112... | collective-permute-start | bytes 835592 | tf_op jit(solution)/shard_map/coefficient_gather_x/ppermute | solution.py:235
  175.8 17.9 %all-to-all-start.9 = ((f32[16,8,128]{2,1,0:T(8,128)}), f32[16,8,128]{2,1,0:T(8,128)}, u32[]{:S(2)}, u32[]{:S(2)}) async-start(f32[16,8,128]{2,1,0:T(8,128)} %broadcast_in_dim.26), calls=%async_computation.9 | async-start | bytes 131072 | tf_op jit(solution)/shard_map/squares/all_to_all | solution.py:96
